TPU v7x, 512 devices: a whole 4x8x8 slice. The times are simulated.
512 devices in a mesh: role: 4 (over x_hi, core), seq: 128 (over z, y, x_lo).
Axes of the slice: x: 4 (x_hi: 2, x_lo: 2; x = x_hi * 2 + x_lo), y: 8, z: 8, core: 2. Of those that a mesh axis runs over, the one named last changes fastest.
Arguments:
- hidden: bfloat16 [16384, 5120], P('seq', 'role'), may hold values from -6 to 6
- gain: float32 [5120], P('role'), may hold values from 0.25 to 1.75
- head_weight: bfloat16 [5120, 64], P('role'), may hold values from -0.078125 to 0.078125
- noise: bfloat16 [16384, 64], P('seq'), may hold values from -6 to 6
- timestep: int32 [1], replicated, may hold values from 100 to 899
- frames: int32 [16384], replicated, may hold values from 0 to 255, never falling along the last dimension, each value on 1 to 128 neighbouring positions
- score_weights: bfloat16 [4, 4, 64, 5120], P('role'), may hold values from -2 to 2
Outputs:
- latent: bfloat16 [16384, 64], P('seq')
- hidden_grad: bfloat16 [16384, 5120], P('seq', 'role')
- head_grad: float32 [5120, 64], P(('role', 'seq'))
- gain_grad: float32 [5120], P(('role', 'seq'))
Inputs may be any that keep to these rules, and one draw needn't show every extreme that they name: `frames`: frame numbers never fall; every frame block has 1 to 128 tokens and one has exactly 128.
All inputs are finite; a program needn't handle non-finite values.
Results may differ from a plain program's by a relative error of at most 0.04.
Values may be sent and summed in bfloat16 or wider, within the bound.
No kernel may reach another device: no remote copies, remote signals or barrier semaphores. Data moves between devices by JAX's collectives and lax.ppermute only.
A program may use at most 64 MiB of HBM per device.

v0:
```python
import math

import jax
import jax.numpy as jnp
from jax import lax
from jax.sharding import PartitionSpec as P

HS = 128


DIFF_TABLE = (-3.0, 2.0, 1.5, -0.5)


def from_behind(block, axis, distance):
    devices = range(lax.axis_size(axis))
    route = [(i - distance, i) for i in devices if i - distance in devices]
    return lax.ppermute(block, axis, route)


def frame_mask(frames, first_row, tok_rows):
    padded = jnp.pad(frames, (2 * tok_rows, 2 * tok_rows))
    query_pos = first_row + jnp.arange(tok_rows, dtype=jnp.int32)
    key_pos = first_row - 2 * tok_rows + jnp.arange(4 * tok_rows, dtype=jnp.int32)
    query_frame = lax.dynamic_slice_in_dim(padded, first_row + 2 * tok_rows, tok_rows, 0)
    key_frame = lax.dynamic_slice_in_dim(padded, first_row, 4 * tok_rows, 0)
    inside = (key_pos >= 0) & (key_pos < frames.shape[0])
    return (
        inside[None, :]
        & (key_frame[None, :] <= query_frame[:, None])
        & (query_pos[:, None] - key_pos[None, :] < 2 * tok_rows)
    )


def attend(query, keys, values, visible):
    heads = query.shape[1] // HS
    query_h = query.reshape(query.shape[0], heads, HS)
    keys_h = keys.reshape(keys.shape[0], heads, HS)
    values_h = values.reshape(values.shape[0], heads, HS)
    scores = jnp.einsum(
        "qhd,khd->hqk", query_h, keys_h, preferred_element_type=jnp.float32
    ) * HS ** (-0.5)
    scores = jnp.where(visible[None], scores, -1e30)
    highest = jnp.max(scores, axis=-1, keepdims=True)
    expo = jnp.exp(scores - highest)
    probabilities = (expo / jnp.sum(expo, axis=-1, keepdims=True)).astype(jnp.bfloat16)
    attended = jnp.einsum(
        "hqk,khd->qhd", probabilities, values_h, preferred_element_type=jnp.float32
    )
    return attended.reshape(query.shape[0], heads * HS).astype(jnp.bfloat16)


def local(hidden, gain, head_weight, noise, timestep, frames, score_weights):
    hidden_f = hidden.astype(jnp.float32)
    gained = (hidden_f * gain).astype(jnp.bfloat16)
    partial_proj = jnp.dot(gained, head_weight, preferred_element_type=jnp.float32)
    squares = jnp.sum(jnp.square(hidden_f), axis=1)
    projected, total_squares = (
        lax.psum(partial_proj.astype(jnp.bfloat16), "role").astype(jnp.float32),
        lax.psum(squares.astype(jnp.bfloat16), "role").astype(jnp.float32),
    )
    full_width = hidden.shape[1] * lax.axis_size("role")
    inverse_rms = lax.rsqrt(total_squares / full_width + 1e-06)
    latent = (inverse_rms[:, None] * projected).astype(jnp.bfloat16)
    phase = 0.5 * math.pi * timestep[0].astype(jnp.float32) / 1000.0
    noisy = (
        jnp.cos(phase) * latent.astype(jnp.float32) + jnp.sin(phase) * noise.astype(jnp.float32)
    ).astype(jnp.bfloat16)
    model_weights = score_weights[0]
    tok_rows = noisy.shape[0]
    first_row = lax.axis_index("seq") * tok_rows
    query = jnp.dot(noisy, model_weights[0], preferred_element_type=jnp.float32).astype(
        jnp.bfloat16
    )
    nearby = {}
    for offset in (2, 1, -1):
        nearby[offset] = from_behind(noisy, "seq", offset)
    window_rows = jnp.concatenate([nearby[2], nearby[1], noisy, nearby[-1]], axis=0)
    keys = jnp.dot(window_rows, model_weights[1], preferred_element_type=jnp.float32).astype(
        jnp.bfloat16
    )
    values = jnp.dot(window_rows, model_weights[2], preferred_element_type=jnp.float32).astype(
        jnp.bfloat16
    )
    visible = frame_mask(frames, first_row, tok_rows)
    attended = attend(query, keys, values, visible)
    predicted = noisy.astype(jnp.float32) + jnp.dot(
        attended, model_weights[3].T, preferred_element_type=jnp.float32
    )
    role_index = lax.axis_index("role")
    weighting = jnp.sum(
        jnp.where(
            jnp.arange(4, dtype=jnp.int32) == role_index, jnp.array(DIFF_TABLE, jnp.float32), 0.0
        )
    )
    score_gap = lax.psum((weighting * predicted).astype(jnp.bfloat16), "role").astype(jnp.float32)
    scaled_grad = (inverse_rms[:, None] * score_gap).astype(jnp.bfloat16)
    gained_grad = jnp.dot(scaled_grad, head_weight.T, preferred_element_type=jnp.float32)
    row_terms = jnp.einsum("tf,tc->fc", gained, scaled_grad, preferred_element_type=jnp.float32)
    gain_terms = jnp.sum(hidden_f * gained_grad, axis=0)
    head_grad, gain_grad = (
        lax.psum_scatter(row_terms, "seq", scatter_dimension=0, tiled=True),
        lax.psum_scatter(gain_terms, "seq", scatter_dimension=0, tiled=True),
    )
    rms_grad = jnp.sum(score_gap * projected, axis=1)
    hidden_grad = (
        gained_grad * gain - (inverse_rms**3 * rms_grad / full_width)[:, None] * hidden_f
    ).astype(jnp.bfloat16)
    return (latent, hidden_grad, head_grad, gain_grad)


def solution(mesh):
    in_specs = (
        P("seq", "role"),
        P("role"),
        P("role", None),
        P("seq", None),
        P(),
        P(),
        P("role", None, None, None),
    )
    out_specs = (P("seq", None), P("seq", "role"), P(("role", "seq"), None), P(("role", "seq")))
    return jax.shard_map(local, mesh=mesh, in_specs=in_specs, out_specs=out_specs, check_vma=False)
```

profile of v0, /device:TPU:2, one launch (start us, length us, event | category | flops | bytes accessed | tf_op | source)
XLA Modules:
  0.0 1220.5 jit_solution(1294447945333339570)
XLA Ops:
  7.2 0.0 copy-start
  7.2 0.0 all-reduce.6.cloned.1.call-start
  8.1 1.1 fusion.16
  9.2 1.2 convolution_convert_fusion.3
  10.4 15.0 %all-reduce.3 = (bf16[128,64]{0,1:T(8,128)(2,1)S(1)}, bf16[128]{0:T(256)(128)(2,1)S(1)}) all-reduce(bf16[128,64]{0,1:T(8,128)(2,1)S(1)} %convolution_convert_fusion.3, bf16[128]{0:T(256)(128)(2,1)S(1)} %fusion.16), channel_id=1, replica_groups=mesh['role'=4,'seq'=128] {'role'}, use_global_device_ids=true, to_apply=%region_2.0 | all-reduce | flops 8320 | bytes 33280 | tf_op jit(solution)/shard_map/psum | solution.py:58
  25.4 1.3 add_convert_fusion
  26.7 3.5 collective-permute-start
  30.2 4.4 collective-permute-start.1
  34.6 1.9 collective-permute-start.2
  36.5 0.8 pad_dynamic-slice_fusion
  37.3 0.8 pad_dynamic-slice_fusion.1
  38.1 2.7 fusion.11
  40.8 0.1 fusion.32
  41.0 1.3 fusion.40
  42.2 1.3 dynamic-slice
  44.2 0.0 collective-permute-done.1
  44.2 0.0 collective-permute-done.2
  44.2 5.0 convolution_convert_fusion.1
  49.1 7.9 copy.18
  57.1 2.7 fusion.9
  59.8 1.5 fusion.2
  61.4 7.3 fusion.47
  68.7 7.2 fusion.10
  75.9 2.1 fusion.15
  78.0 13.1 %psum.23 = bf16[128,64]{0,1:T(8,128)(2,1)S(1)} all-reduce(bf16[128,64]{0,1:T(8,128)(2,1)S(1)} %fusion.15), channel_id=1, replica_groups=mesh['role'=4,'seq'=128] {'role'}, use_global_device_ids=true, to_apply=%region_6.7 | all-reduce | flops 8192 | bytes 32768 | tf_op jit(solution)/shard_map/psum | solution.py:95
  91.1 1.1 fusion.29
  92.3 0.0 all-reduce.6.cloned.1.call-update
  92.3 1.1 fusion.20
  93.4 314.4 %all-reduce.2 = f32[1280]{0:T(1024)S(1)} all-reduce(f32[1280]{0:T(1024)S(1)} %get-tuple-element.8), channel_id=3, replica_groups=mesh['role'=4,'seq'=128] {'seq'}, use_global_device_ids=true, to_apply=%region_10.11.clone | all-reduce | flops 1280 | bytes 10240
  407.8 0.6 dynamic-slice.3
  408.4 803.9 %all-reduce.6.cloned.1.call-done = f32[1280,64]{1,0:T(8,128)} async-done(((f32[1280,64]{1,0:T(8,128)}), f32[1280,64]{1,0:T(8,128)}) %all-reduce.6.cloned.1.call-update) | async-done | bytes 327696
  1212.4 1.3 constant_dynamic-slice_fusion
  (12 shorter events, 0.1 us)
Async XLA Ops:
  7.2 2.0 copy-start
  7.2 1205.2 %all-reduce.6.cloned.1.call-start = ((), (), s32[]{:S(2)}) async-start(), calls=%async_computation | async-start | bytes 1310720
  26.7 17.4 %collective-permute-start = (bf16[128,64]{0,1:T(8,128)(2,1)S(1)}, bf16[128,64]{0,1:T(8,128)(2,1)S(1)}, u32[]{:S(2)}, u32[]{:S(2)}) collective-permute-start(bf16[128,64]{0,1:T(8,128)(2,1)S(1)} %get-tuple-element.6), channel_id=1, source_target_pairs={{0,2},{1,3},{2,4},{3,5},{4,6},{5,7},{6,8},{7,9},{8,10},{9,11},{10,... | collective-permute-start | bytes 49160 | tf_op jit(solution)/shard_map/ppermute | solution.py:17
  30.2 13.9 %collective-permute-start.1 = (bf16[128,64]{0,1:T(8,128)(2,1)S(1)}, bf16[128,64]{0,1:T(8,128)(2,1)S(1)}, u32[]{:S(2)}, u32[]{:S(2)}) collective-permute-start(bf16[128,64]{0,1:T(8,128)(2,1)S(1)} %get-tuple-element.6), channel_id=1, source_target_pairs={{0,1},{1,2},{2,3},{3,4},{4,5},{5,6},{6,7},{7,8},{8,9},{9,10},{10,1... | collective-permute-start | bytes 49160 | tf_op jit(solution)/shard_map/ppermute | solution.py:17
  34.6 9.6 collective-permute-start.2
  57.1 2.7 copy-start.1
  68.6 22.5 %copy-start.2 = (bf16[128,1280]{1,0:T(8,128)(2,1)S(1)}, bf16[128,1280]{1,0:T(8,128)(2,1)}, u32[]{:S(2)}) copy-start(bf16[128,1280]{1,0:T(8,128)(2,1)} %param.8) | copy-start | bytes 983044
  68.7 22.5 %copy-start.3 = (f32[1280]{0:T(1024)S(1)}, f32[1280]{0:T(1024)}, u32[]{:S(2)}) copy-start(f32[1280]{0:T(1024)} %param.9) | copy-start | bytes 15364
Sparse Core Ops, SparseCore 0:
  92.4 1119.8 all-reduce.5
where the time goes:
time: 1220 us
  waiting for transfers between devices  804 us (66%)
  blocking collectives  343 us (28%)
  matrix products  24.7 us (2%)
  between operations  15.6 us (1%)
  other arithmetic  12.8 us (1%)
    unnamed x2, waiting for transfers between devices  804 us
    unnamed x1, blocking collectives  314 us
  transfers between devices with their start and end apart: 4, of which 1 were waited for; matrix products, arithmetic and copies ran while one was open for 1% of the time, Pallas kernels for 0%

commit v1 on v0

v1 whole, which is shorter than its diff:
```python
import functools
import math

import jax
import jax.numpy as jnp
from jax import lax
from jax.experimental import pallas as pl
from jax.experimental.pallas import tpu as pltpu
from jax.sharding import PartitionSpec as P

HS = 128
DIFF_TABLE = (-3.0, 2.0, 1.5, -0.5)
BF = jnp.bfloat16
F32 = jnp.float32
NN = (((1,), (0,)), ((), ()))
NT = (((1,), (1,)), ((), ()))
TN = (((0,), (0,)), ((), ()))
SENT_ROWS = 80
PARAMS = pltpu.CompilerParams(vmem_limit_bytes=40 * 1024 * 1024)


def from_behind(block, axis, distance):
    devices = range(lax.axis_size(axis))
    route = [(i - distance, i) for i in devices if i - distance in devices]
    return lax.ppermute(block, axis, route)


def mm(a, b, dims=NN):
    return lax.dot_general(a, b, dims, preferred_element_type=F32)


def call(body, outs, *args, specs=None, flops=0, scratch=()):
    read = sum(a.size * a.dtype.itemsize for a in args)
    return pl.pallas_call(
        body,
        out_shape=outs,
        in_specs=specs or [pl.BlockSpec(memory_space=pltpu.VMEM)] * len(args),
        scratch_shapes=list(scratch),
        compiler_params=PARAMS,
        cost_estimate=pl.CostEstimate(flops=flops, bytes_accessed=read, transcendentals=0),
    )(*args)


def project_body(hidden_ref, gain_ref, head_ref, out_ref):
    hidden = hidden_ref[...].astype(F32)
    gained = (hidden * gain_ref[...]).astype(BF)
    out_ref[0:64, :] = mm(head_ref[...], gained, NT).astype(BF)
    squares = hidden * hidden
    lanes = functools.reduce(
        jnp.add, [squares[:, i : i + 128] for i in range(0, squares.shape[1], 128)]
    )
    total = jnp.sum(lanes.T, axis=0, keepdims=True)
    high = total.astype(BF).astype(F32)
    row = lax.broadcasted_iota(jnp.int32, (16, 128), 0)
    out_ref[64:80, :] = jnp.where(row == 0, high, jnp.where(row == 1, total - high, 0.0)).astype(BF)


def noisy_body(width, parts_ref, noise_ref, mix_ref, proj_ref, inv_ref, latent_ref, noisy_ref):
    total = jnp.sum(parts_ref[...].astype(F32), axis=0)
    projected = total[0:64]
    inverse = lax.rsqrt((total[64:65] + total[65:66]) / width + 1e-06)
    proj_ref[...] = projected
    inv_ref[...] = inverse
    latent = (inverse * projected).astype(BF)
    latent_ref[...] = latent
    noisy_ref[...] = (
        mix_ref[0] * latent.astype(F32) + mix_ref[1] * noise_ref[...].astype(F32)
    ).astype(BF)


def prepare_body(place_ref, w_ref, frames_ref, hidden_ref, fold_ref, join_ref, bias_ref, spread_ref):
    scale = HS ** (-0.5) * math.log2(math.e)
    heads = w_ref.shape[3] // HS
    zero = jnp.zeros((64, HS), BF)
    for h in range(heads):
        cols = slice(h * HS, (h + 1) * HS)
        fold_ref[h * 64 : (h + 1) * 64, :] = (
            mm(w_ref[0, 1, :, cols], w_ref[0, 0, :, cols], NT) * scale
        ).astype(BF)
    for h in range(0, heads, 2):
        one, two = slice(h * HS, (h + 1) * HS), slice((h + 1) * HS, (h + 2) * HS)
        values = jnp.concatenate(
            [
                jnp.concatenate([w_ref[0, 2, :, one], zero], axis=1),
                jnp.concatenate([zero, w_ref[0, 2, :, two]], axis=1),
            ],
            axis=0,
        )
        join_ref[:, h * 64 : (h + 2) * 64] = mm(
            w_ref[0, 3, :, h * HS : (h + 2) * HS], values, NT
        ).astype(BF)
    place = place_ref[0]
    blocks = frames_ref.shape[0]
    query_frame = frames_ref[pl.ds(place, 1), :]
    ahead = lax.broadcasted_iota(jnp.int32, (128, 128), 0)
    token = lax.broadcasted_iota(jnp.int32, (128, 128), 1)
    for b, offset in enumerate((-2, -1, 0, 1)):
        block = place + offset
        held = jnp.clip(block, 0, blocks - 1)
        key_frame = jnp.broadcast_to(frames_ref[pl.ds(held, 1), :], (128, 128)).T
        key = ahead + offset * 128
        seen = (key_frame <= query_frame) & (token - key < 256)
        seen = seen & (block >= 0) & (block < blocks)
        bias_ref[b * 128 : (b + 1) * 128, :] = jnp.where(seen, 0.0, -1e30).astype(BF)
    features = hidden_ref.shape[1]
    to = lax.broadcasted_iota(jnp.int32, (256, 320), 0)
    source = lax.broadcasted_iota(jnp.int32, (256, 320), 1)
    slot = to & 7
    want = (to >> 3) * 10 + slot
    first = jnp.where((slot < 5) & (source == want), 1.0, 0.0).astype(BF)
    second = jnp.where((slot < 5) & (source == want + 5), 1.0, 0.0).astype(BF)
    for i in range(features // 320):
        piece = hidden_ref[:, i * 320 : (i + 1) * 320]
        rows = slice(i * 256, (i + 1) * 256)
        spread_ref[rows, 0:128] = mm(first, piece, NT).astype(BF)
        spread_ref[rows, 128:256] = mm(second, piece, NT).astype(BF)


def attend_body(
    weight_ref, before2_ref, before1_ref, own_ref, after_ref, fold_ref, join_ref, bias_ref, out_ref,
    query_ref, mixed_ref,
):
    heads = fold_ref.shape[0] // 64
    own = own_ref[...]
    window = jnp.concatenate([before2_ref[...], before1_ref[...], own, after_ref[...]], axis=1)
    row = lax.broadcasted_iota(jnp.int32, (16, 512), 0)
    summing = jnp.concatenate([window, jnp.where(row == 0, 1.0, 0.0).astype(BF)], axis=0)
    keys = jnp.concatenate([window.astype(F32).T.astype(BF), bias_ref[...]], axis=1)
    query_ref[...] = mm(fold_ref[...], own).astype(BF)
    eye = (
        lax.broadcasted_iota(jnp.int32, (128, 128), 0) == lax.broadcasted_iota(jnp.int32, (128, 128), 1)
    )
    eye = jnp.where(eye, 1.0, 0.0).astype(BF)
    eyes = jnp.concatenate([eye, eye], axis=1)
    for h in range(0, heads, 2):
        pair = jnp.concatenate(
            [query_ref[h * 64 : (h + 1) * 64, :], query_ref[(h + 1) * 64 : (h + 2) * 64, :]], axis=1
        )
        scores = mm(keys, jnp.concatenate([pair, eyes], axis=0))
        highest = jnp.max(scores, axis=0, keepdims=True)
        expo = jnp.exp2(scores - highest).astype(BF)
        mixed = mm(summing, expo)
        normal = (mixed[0:64] / mixed[64:65]).astype(BF)
        mixed_ref[h * 64 : (h + 1) * 64, :] = normal[:, 0:128]
        mixed_ref[(h + 1) * 64 : (h + 2) * 64, :] = normal[:, 128:256]
    predicted = own.astype(F32) + mm(join_ref[...], mixed_ref[...])
    out_ref[...] = (weight_ref[0] * predicted).astype(BF)


def gap_body(parts_ref, inv_ref, spread_ref, gap_ref, scaled_ref, terms_ref):
    gap = jnp.sum(parts_ref[...].astype(F32), axis=0)
    gap_ref[...] = gap
    scaled = (inv_ref[...] * gap).astype(BF)
    scaled_ref[...] = scaled
    zero = jnp.zeros_like(scaled)
    both = jnp.concatenate(
        [jnp.concatenate([scaled, zero], axis=1), jnp.concatenate([zero, scaled], axis=1)], axis=0
    )
    terms = mm(spread_ref[...], both, NT)
    terms_ref[...] = terms.reshape(terms_ref.shape).astype(BF)


def hidden_grad_body(
    width, gap_ref, proj_ref, inv_ref, scaled_ref, head_ref, gain_ref, hidden_ref, out_ref
):
    inverse = inv_ref[...]
    rms_grad = jnp.sum(gap_ref[...] * proj_ref[...], axis=0, keepdims=True)
    pull = inverse * inverse * inverse * rms_grad / width
    column = jnp.broadcast_to(pull, (128, 128)).T[:, 0:1]
    gained_grad = mm(scaled_ref[...], head_ref[...], TN)
    out_ref[...] = (
        gained_grad * gain_ref[...] - column * hidden_ref[...].astype(F32)
    ).astype(BF)


def finish_body(terms_ref, gain_ref, head_ref, head_grad_ref, gain_grad_ref):
    total = jnp.sum(terms_ref[...].astype(F32), axis=0)
    rows = jnp.concatenate([total[0:5, 0:64], total[0:5, 64:128]], axis=0)
    head_grad_ref[...] = gain_ref[...] * rows
    gain_grad_ref[...] = jnp.sum(head_ref[...].astype(F32) * rows, axis=1, keepdims=True)


def local(hidden, gain, head_weight, noise, timestep, frames, score_weights):
    shape = jax.ShapeDtypeStruct
    smem, vmem = pl.BlockSpec(memory_space=pltpu.SMEM), pl.BlockSpec(memory_space=pltpu.VMEM)
    tok_rows, features = hidden.shape
    width = features * lax.axis_size("role")
    blocks = lax.axis_size("seq")
    head_t = head_weight.T
    gain_row = gain[None, :]
    place = lax.axis_index("seq").astype(jnp.int32)
    role_index = lax.axis_index("role")
    weighting = jnp.sum(
        jnp.where(jnp.arange(4, dtype=jnp.int32) == role_index, jnp.array(DIFF_TABLE, F32), 0.0)
    )
    phase = 0.5 * math.pi * timestep[0].astype(F32) / 1000.0
    mix = jnp.stack([jnp.cos(phase), jnp.sin(phase)])

    sent = call(project_body, shape((SENT_ROWS, tok_rows), BF), hidden, gain_row, head_t)
    parts = lax.all_gather(sent, "role")
    projected, inverse, latent, noisy = call(
        functools.partial(noisy_body, width),
        (shape((64, tok_rows), F32), shape((1, tok_rows), F32), shape((64, tok_rows), BF), shape((64, tok_rows), BF)),
        parts, noise.T, mix, specs=[vmem, vmem, smem],
    )
    near = [from_behind(noisy, "seq", offset) for offset in (2, 1, -1)]
    fold, join, bias, spread = call(
        prepare_body,
        (shape((2560, 64), BF), shape((64, 2560), BF), shape((512, 128), BF), shape((blocks * 8, 256), BF)),
        place[None], score_weights, frames.reshape(blocks, tok_rows), hidden,
        specs=[smem, vmem, vmem, vmem], flops=2_000_000_000,
    )
    predicted = call(
        attend_body, shape((64, tok_rows), BF),
        weighting[None], near[0], near[1], noisy, near[2], fold, join, bias,
        specs=[smem] + [vmem] * 7, flops=3_000_000_000,
        scratch=[pltpu.VMEM((2560, 128), BF), pltpu.VMEM((2560, 128), BF)],
    )
    gaps = lax.all_gather(predicted, "role")
    gap, scaled, terms = call(
        gap_body,
        (shape((64, tok_rows), F32), shape((64, tok_rows), BF), shape((blocks, 8, 128), BF)),
        gaps, inverse, spread,
    )
    summed = lax.all_to_all(terms, "seq", 0, 0)
    hidden_grad = call(
        functools.partial(hidden_grad_body, width), shape(hidden.shape, BF),
        gap, projected, inverse, scaled, head_t, gain_row, hidden, flops=1_000_000_000,
    )
    own_gain = lax.dynamic_slice_in_dim(gain, place * 10, 10, 0)
    own_head = lax.dynamic_slice_in_dim(head_weight, place * 10, 10, 0)
    head_grad, gain_grad = call(
        finish_body, (shape((10, 64), F32), shape((10, 1), F32)), summed, own_gain[:, None], own_head
    )
    return (latent.T, hidden_grad, head_grad, gain_grad[:, 0])


def solution(mesh):
    in_specs = (
        P("seq", "role"),
        P("role"),
        P("role", None),
        P("seq", None),
        P(),
        P(),
        P("role", None, None, None),
    )
    out_specs = (P("seq", None), P("seq", "role"), P(("role", "seq"), None), P(("role", "seq")))
    return jax.shard_map(local, mesh=mesh, in_specs=in_specs, out_specs=out_specs, check_vma=False)
```

time: 1220 us -> 80.9 us (0.07)
  the two profiles are of different devices: /device:TPU:2 before, /device:TPU:4 now
where the time goes in v1:
time: 80.9 us; the launch traced here: 80.3 us
  starting transfers between devices  26 us (32%)
  blocking collectives  15.9 us (20%)
  Pallas kernels  14.6 us (18%)
  waiting for transfers between devices  13 us (16%)
  local copies, waits for them, and re-layouts  7.93 us (10%)
  between operations  1.54 us (2%)
  other arithmetic  1.3 us (2%)
    all_to_all x1, starting transfers between devices, local(): summed = lax.all_to_all(terms, 'seq', 0, 0)  20.5 us
    pallas_call x7, Pallas kernels, call(): pl.pallas_call(body, out_shape=outs, in_specs=specs or [pl.BlockSpec(memo...  14.6 us
    all_to_all x1, waiting for transfers between devices, local(): summed = lax.all_to_all(terms, 'seq', 0, 0)  13 us
    all_gather x1, blocking collectives, local(): parts = lax.all_gather(sent, 'role')  9.15 us
    all_gather x1, blocking collectives, local(): gaps = lax.all_gather(predicted, 'role')  6.75 us
    unnamed x19, local copies, waits for them, and re-layouts  6.24 us
    ppermute x3, starting transfers between devices, from_behind(): return lax.ppermute(block, axis, route)  5.5 us
  transfers between devices with their start and end apart: 4, of which 1 were waited for; matrix products, arithmetic and copies ran while one was open for 2% of the time, Pallas kernels for 3%

profile of v1, /device:TPU:4, one launch (start us, length us, event | category | flops | bytes accessed | tf_op | source)
XLA Modules:
  0.0 80.3 jit_solution(7269893092137097092)
XLA Ops:
  1.4 0.7 broadcast_in_dim.16.gain_ref
  2.1 1.0 %copy-done = bf16[128,1280]{1,0:T(8,128)(2,1)S(1)} copy-done((bf16[128,1280]{1,0:T(8,128)(2,1)S(1)}, bf16[128,1280]{1,0:T(8,128)(2,1)}, u32[]{:S(2)}) %copy-start) | copy-done | bytes 327704
  3.1 0.9 %copy-done.3 = bf16[1280,64]{0,1:T(8,128)(2,1)S(1)} copy-done((bf16[1280,64]{0,1:T(8,128)(2,1)S(1)}, bf16[1280,64]{0,1:T(8,128)(2,1)}, u32[]{:S(2)}) %copy-start.3) | copy-done | bytes 163864
  4.0 0.3 shard_map.111
  4.3 9.1 %all-gather = bf16[320,128]{1,0:T(8,128)(2,1)S(1)} all-gather(bf16[80,128]{1,0:T(8,128)(2,1)S(1)} %shard_map.111), channel_id=2, replica_groups=mesh['role'=4,'seq'=128] {'role'}, dimensions={0}, use_global_device_ids=true | all-gather | bytes 102400 | tf_op jit(solution)/shard_map/all_gather | solution.py:200
  13.4 0.1 pad_maximum_fusion.mix_ref
  13.5 0.7 copy-done.5
  14.2 1.2 %shard_map.112 = (f32[64,128]{1,0:T(8,128)S(1)}, f32[1,128]{1,0:T(1,128)S(1)}, bf16[64,128]{1,0:T(8,128)(2,1)}, bf16[64,128]{1,0:T(8,128)(2,1)S(1)}) custom-call(bf16[4,80,128]{2,1,0:T(8,128)(2,1)S(1)} %bitcast.10, bf16[64,128]{1,0:T(8,128)(2,1)S(1)} %bitcast.14, f32[2]{0:T(128)S(1)} %pad_maximum_fusion.mix_ref), custom_call_target="tpu_custom_call" | custom-call | bytes 98312 | tf_op jit(solution)/shard_map/pallas_call | solution.py:34
  15.4 1.3 %collective-permute-start = (bf16[64,128]{1,0:T(8,128)(2,1)S(1)}, bf16[64,128]{1,0:T(8,128)(2,1)S(1)}, u32[]{:S(2)}, u32[]{:S(2)}) collective-permute-start(bf16[64,128]{1,0:T(8,128)(2,1)S(1)} %get-tuple-element.18.own_ref), channel_id=1, source_target_pairs={{0,2},{1,3},{2,4},{3,5},{4,6},{5,7},{6,8},{7,9},{8,10},{9,11},{10,... | collective-permute-start | bytes 49160 | tf_op jit(solution)/shard_map/ppermute | solution.py:25
  16.7 2.9 %collective-permute-start.1 = (bf16[64,128]{1,0:T(8,128)(2,1)S(1)}, bf16[64,128]{1,0:T(8,128)(2,1)S(1)}, u32[]{:S(2)}, u32[]{:S(2)}) collective-permute-start(bf16[64,128]{1,0:T(8,128)(2,1)S(1)} %get-tuple-element.18.own_ref), channel_id=1, source_target_pairs={{0,1},{1,2},{2,3},{3,4},{4,5},{5,6},{6,7},{7,8},{8,9},{9,10},{10,1... | collective-permute-start | bytes 49160 | tf_op jit(solution)/shard_map/ppermute | solution.py:25
  19.6 1.3 %collective-permute-start.2 = (bf16[64,128]{1,0:T(8,128)(2,1)S(1)}, bf16[64,128]{1,0:T(8,128)(2,1)S(1)}, u32[]{:S(2)}, u32[]{:S(2)}) collective-permute-start(bf16[64,128]{1,0:T(8,128)(2,1)S(1)} %get-tuple-element.18.own_ref), channel_id=1, source_target_pairs={{1,0},{2,1},{3,2},{4,3},{5,4},{6,5},{7,6},{8,7},{9,8},{10,9},{11,1... | collective-permute-start | bytes 49160 | tf_op jit(solution)/shard_map/ppermute | solution.py:25
  20.9 0.0 copy-start.1
  20.9 1.0 %copy-done.1 = bf16[128,1280]{1,0:T(8,128)(2,1)S(1)} copy-done((bf16[128,1280]{1,0:T(8,128)(2,1)S(1)}, bf16[128,1280]{1,0:T(8,128)(2,1)}, u32[]{:S(2)}) %copy-start.1) | copy-done | bytes 327704
  21.9 1.7 %copy-done.6 = bf16[1,4,64,5120]{3,2,1,0:T(8,128)(2,1)S(1)} copy-done((bf16[1,4,64,5120]{3,2,1,0:T(8,128)(2,1)S(1)}, bf16[1,4,64,5120]{3,2,1,0:T(8,128)(2,1)}, u32[]{:S(2)}) %copy-start.6) | copy-done | bytes 2621464
  23.6 0.8 %copy-done.7 = s32[16384]{0:T(1024)S(1)} copy-done((s32[16384]{0:T(1024)S(1)}, s32[16384]{0:T(1024)}, u32[]{:S(2)}) %copy-start.7) | copy-done | bytes 65560
  24.5 1.4 %shard_map.113 = (bf16[2560,64]{1,0:T(8,128)(2,1)S(1)}, bf16[64,2560]{1,0:T(8,128)(2,1)S(1)}, bf16[512,128]{1,0:T(8,128)(2,1)S(1)}, bf16[1024,256]{1,0:T(8,128)(2,1)S(1)}) custom-call(s32[1]{0:T(128)} %bitcast.5.place_ref, bf16[1,4,64,5120]{3,2,1,0:T(8,128)(2,1)S(1)} %copy-done.6, s32[128,128]{1,0:T(8,128)S(1)} %bitcast.15, bf16[128,1280]{1,0:T(8,128)(2,1)S(1)} %copy-done.1), custom_call_target="tpu_custom_call" | custom-call | flops 2000000000 | bytes 3014660 | tf_op jit(solution)/shard_map/pallas_call | solution.py:34
  25.9 0.6 fusion
  26.5 0.0 collective-permute-done.before2_ref
  26.5 0.0 copy-start.4
  26.5 0.0 copy-start.2
  26.5 8.9 %shard_map.114 = bf16[64,128]{1,0:T(8,128)(2,1)S(1)} custom-call(f32[1]{0:T(128)} %bitcast.4.weight_ref, bf16[64,128]{1,0:T(8,128)(2,1)S(1)} %collective-permute-done.before2_ref, bf16[64,128]{1,0:T(8,128)(2,1)S(1)} %collective-permute-done.1.before1_ref, bf16[64,128]{1,0:T(8,128)(2,1)S(1)} %get-tuple-element.18.own_ref, ...), custom_call_target="tpu_custom_call" | custom-call | flops 3000000000 | bytes 851972 | tf_op jit(solution)/shard_map/pallas_call | solution.py:34
  35.4 6.8 %all-gather.1 = bf16[256,128]{1,0:T(8,128)(2,1)S(1)} all-gather(bf16[64,128]{1,0:T(8,128)(2,1)S(1)} %shard_map.114), channel_id=3, replica_groups=mesh['role'=4,'seq'=128] {'role'}, dimensions={0}, use_global_device_ids=true | all-gather | bytes 81920 | tf_op jit(solution)/shard_map/all_gather | solution.py:219
  42.2 1.0 %shard_map.115 = (f32[64,128]{1,0:T(8,128)S(1)}, bf16[64,128]{1,0:T(8,128)(2,1)S(1)}, bf16[128,8,128]{2,1,0:T(8,128)(2,1)}) custom-call(bf16[4,64,128]{2,1,0:T(8,128)(2,1)S(1)} %bitcast.11, f32[1,128]{1,0:T(1,128)S(1)} %get-tuple-element.22.inv_ref, bf16[1024,256]{1,0:T(8,128)(2,1)S(1)} %get-tuple-element.23.spread_ref), custom_call_target="tpu_custom_call" | custom-call | bytes 590336 | tf_op jit(solution)/shard_map/pallas_call | solution.py:34
  43.2 20.5 %all-to-all-start = ((bf16[128,8,128]{2,1,0:T(8,128)(2,1)}), bf16[128,8,128]{2,1,0:T(8,128)(2,1)S(1)}, u32[]{:S(2)}, u32[]{:S(2)}) async-start(bf16[128,8,128]{2,1,0:T(8,128)(2,1)} %get-tuple-element.27), calls=%async_computation | async-start | bytes 524288 | tf_op jit(solution)/shard_map/all_to_all | solution.py:225
  63.7 0.1 constant_dynamic-slice_fusion
  63.8 0.1 copy.16.head_ref
  63.9 0.8 dynamic-slice_bitcast_fusion
  64.7 0.1 copy.15.gain_ref
  64.8 1.0 %shard_map.116 = bf16[128,1280]{1,0:T(8,128)(2,1)} custom-call(f32[64,128]{1,0:T(8,128)S(1)} %get-tuple-element.24.gap_ref, f32[64,128]{1,0:T(8,128)S(1)} %get-tuple-element.25.proj_ref, f32[1,128]{1,0:T(1,128)S(1)} %get-tuple-element.22.inv_ref, bf16[64,128]{1,0:T(8,128)(2,1)S(1)} %get-tuple-element.26.scaled_ref, bf16[64,1280]{1,0:T(8,128)(2,1)S(1)} %bitcast.13, ...), custom_call_target="tpu_custom_call" | custom-call | flops 1000000000 | bytes 579072 | tf_op jit(solution)/shard_map/pallas_call | solution.py:34
  65.8 13.0 %all-to-all-done.terms_ref = bf16[128,8,128]{2,1,0:T(8,128)(2,1)S(1)} async-done(((bf16[128,8,128]{2,1,0:T(8,128)(2,1)}), bf16[128,8,128]{2,1,0:T(8,128)(2,1)S(1)}, u32[]{:S(2)}, u32[]{:S(2)}) %all-to-all-start) | async-done | bytes 262176 | tf_op jit(solution)/shard_map/all_to_all | solution.py:225
  78.8 0.9 %shard_map.117 = (f32[10,64]{1,0:T(8,128)}, f32[10,1]{1,0:T(8,128)S(1)}) custom-call(bf16[128,8,128]{2,1,0:T(8,128)(2,1)S(1)} %all-to-all-done.terms_ref, f32[10,1]{1,0:T(8,128)S(1)} %copy.15.gain_ref, bf16[10,64]{1,0:T(8,128)(2,1)S(1)} %copy.16.head_ref), custom_call_target="tpu_custom_call" | custom-call | bytes 263464 | tf_op jit(solution)/shard_map/pallas_call | solution.py:34
  79.7 0.6 reduce
  (11 shorter events, 0.0 us)
Async XLA Ops:
  2.1 1.0 %copy-start = (bf16[128,1280]{1,0:T(8,128)(2,1)S(1)}, bf16[128,1280]{1,0:T(8,128)(2,1)}, u32[]{:S(2)}) copy-start(bf16[128,1280]{1,0:T(8,128)(2,1)} %hidden_ref.5) | copy-start | bytes 983044
  3.1 0.9 %copy-start.3 = (bf16[1280,64]{0,1:T(8,128)(2,1)S(1)}, bf16[1280,64]{0,1:T(8,128)(2,1)}, u32[]{:S(2)}) copy-start(bf16[1280,64]{0,1:T(8,128)(2,1)} %param.10) | copy-start | bytes 491524
  13.5 0.7 copy-start.5
  15.4 11.1 %collective-permute-start = (bf16[64,128]{1,0:T(8,128)(2,1)S(1)}, bf16[64,128]{1,0:T(8,128)(2,1)S(1)}, u32[]{:S(2)}, u32[]{:S(2)}) collective-permute-start(bf16[64,128]{1,0:T(8,128)(2,1)S(1)} %get-tuple-element.18.own_ref), channel_id=1, source_target_pairs={{0,2},{1,3},{2,4},{3,5},{4,6},{5,7},{6,8},{7,9},{8,10},{9,11},{10,... | collective-permute-start | bytes 49160 | tf_op jit(solution)/shard_map/ppermute | solution.py:25
  16.7 9.8 %collective-permute-start.1 = (bf16[64,128]{1,0:T(8,128)(2,1)S(1)}, bf16[64,128]{1,0:T(8,128)(2,1)S(1)}, u32[]{:S(2)}, u32[]{:S(2)}) collective-permute-start(bf16[64,128]{1,0:T(8,128)(2,1)S(1)} %get-tuple-element.18.own_ref), channel_id=1, source_target_pairs={{0,1},{1,2},{2,3},{3,4},{4,5},{5,6},{6,7},{7,8},{8,9},{9,10},{10,1... | collective-permute-start | bytes 49160 | tf_op jit(solution)/shard_map/ppermute | solution.py:25
  19.6 6.9 %collective-permute-start.2 = (bf16[64,128]{1,0:T(8,128)(2,1)S(1)}, bf16[64,128]{1,0:T(8,128)(2,1)S(1)}, u32[]{:S(2)}, u32[]{:S(2)}) collective-permute-start(bf16[64,128]{1,0:T(8,128)(2,1)S(1)} %get-tuple-element.18.own_ref), channel_id=1, source_target_pairs={{1,0},{2,1},{3,2},{4,3},{5,4},{6,5},{7,6},{8,7},{9,8},{10,9},{11,1... | collective-permute-start | bytes 49160 | tf_op jit(solution)/shard_map/ppermute | solution.py:25
  20.9 1.0 %copy-start.1 = (bf16[128,1280]{1,0:T(8,128)(2,1)S(1)}, bf16[128,1280]{1,0:T(8,128)(2,1)}, u32[]{:S(2)}) copy-start(bf16[128,1280]{1,0:T(8,128)(2,1)} %hidden_ref.5) | copy-start | bytes 983044
  21.9 1.7 %copy-start.6 = (bf16[1,4,64,5120]{3,2,1,0:T(8,128)(2,1)S(1)}, bf16[1,4,64,5120]{3,2,1,0:T(8,128)(2,1)}, u32[]{:S(2)}) copy-start(bf16[1,4,64,5120]{3,2,1,0:T(8,128)(2,1)} %w_ref.1) | copy-start | bytes 7864324
  23.6 0.8 %copy-start.7 = (s32[16384]{0:T(1024)S(1)}, s32[16384]{0:T(1024)}, u32[]{:S(2)}) copy-start(s32[16384]{0:T(1024)} %param.13) | copy-start | bytes 196612
  24.5 1.4 %copy-start.8 = (f32[4]{0:T(128)S(1)}, f32[4]{0:T(128)}, u32[]{:S(2)}) copy-start(f32[4]{0:T(128)} %constant.25.clone) | copy-start | bytes 52
  26.5 37.2 %copy-start.4 = (bf16[1280,64]{0,1:T(8,128)(2,1)S(1)}, bf16[1280,64]{0,1:T(8,128)(2,1)}, u32[]{:S(2)}) copy-start(bf16[1280,64]{0,1:T(8,128)(2,1)} %param.10) | copy-start | bytes 491524
  26.5 38.2 %copy-start.2 = (bf16[128,1280]{1,0:T(8,128)(2,1)S(1)}, bf16[128,1280]{1,0:T(8,128)(2,1)}, u32[]{:S(2)}) copy-start(bf16[128,1280]{1,0:T(8,128)(2,1)} %hidden_ref.5) | copy-start | bytes 983044
  43.2 35.6 %all-to-all-start = ((bf16[128,8,128]{2,1,0:T(8,128)(2,1)}), bf16[128,8,128]{2,1,0:T(8,128)(2,1)S(1)}, u32[]{:S(2)}, u32[]{:S(2)}) async-start(bf16[128,8,128]{2,1,0:T(8,128)(2,1)} %get-tuple-element.27), calls=%async_computation | async-start | bytes 524288 | tf_op jit(solution)/shard_map/all_to_all | solution.py:225

commit v2 on v1

v2 whole, which is shorter than its diff:
```python
import functools
import math

import jax
import jax.numpy as jnp
from jax import lax
from jax.experimental import pallas as pl
from jax.experimental.pallas import tpu as pltpu
from jax.sharding import PartitionSpec as P

HS = 128
DIFF_TABLE = (-3.0, 2.0, 1.5, -0.5)
BF = jnp.bfloat16
F32 = jnp.float32
NN = (((1,), (0,)), ((), ()))
NT = (((1,), (1,)), ((), ()))
TN = (((0,), (0,)), ((), ()))
SENT_ROWS = 80
GROUP = 4
VMEM, SMEM = pl.BlockSpec(memory_space=pltpu.VMEM), pl.BlockSpec(memory_space=pltpu.SMEM)
HBM = pl.BlockSpec(memory_space=pltpu.HBM)


def from_behind(block, axis, distance):
    devices = range(lax.axis_size(axis))
    route = [(i - distance, i) for i in devices if i - distance in devices]
    return lax.ppermute(block, axis, route)


def mm(a, b, dims=NN):
    return lax.dot_general(a, b, dims, preferred_element_type=F32)


def call(body, outs, *args, specs=None, flops=0, scratch=(), limit=8):
    read = sum(a.size * a.dtype.itemsize for a in args)
    return pl.pallas_call(
        body,
        out_shape=outs,
        in_specs=specs or [VMEM] * len(args),
        scratch_shapes=list(scratch),
        compiler_params=pltpu.CompilerParams(vmem_limit_bytes=limit * 1024 * 1024),
        cost_estimate=pl.CostEstimate(flops=flops, bytes_accessed=read, transcendentals=0),
    )(*args)


def in_hbm(array):
    return pltpu.with_memory_space_constraint(array, pltpu.HBM)


def fetch(pairs, sems):
    copies = [pltpu.make_async_copy(a, b, sems.at[i]) for i, (a, b) in enumerate(pairs)]
    for copy in copies:
        copy.start()
    return copies


def project_body(
    hidden_hbm, gain_hbm, head_hbm, noise_hbm, out_ref, noise_ref, hidden_ref, gain_ref, head_ref,
    sems,
):
    features = hidden_ref.shape[1]
    pieces = [slice(i, i + 256) for i in range(0, features, 256)]
    copies = fetch(
        [(gain_hbm, gain_ref)]
        + [(hidden_hbm.at[:, piece], hidden_ref.at[:, piece]) for piece in pieces]
        + [(head_hbm, head_ref), (noise_hbm, noise_ref)],
        sems,
    )
    copies[0].wait()
    gained, lanes = [], 0.0
    for i in range(features // 128):
        if i % 2 == 0:
            copies[1 + i // 2].wait()
        hidden = hidden_ref[:, i * 128 : (i + 1) * 128].astype(F32)
        gained.append((hidden * gain_ref[i : i + 1, :]).astype(BF))
        lanes = lanes + hidden * hidden
    copies[-2].wait()
    out_ref[0:64, :] = mm(head_ref[...], jnp.concatenate(gained, axis=1), NT).astype(BF)
    total = jnp.sum(lanes.T, axis=0, keepdims=True)
    high = total.astype(BF).astype(F32)
    row = lax.broadcasted_iota(jnp.int32, (16, 128), 0)
    out_ref[64:80, :] = jnp.where(row == 0, high, jnp.where(row == 1, total - high, 0.0)).astype(BF)
    copies[-1].wait()


def noisy_body(width, parts_ref, noise_ref, cos_ref, sin_ref, proj_ref, inv_ref, noisy_ref):
    total = jnp.sum(parts_ref[...].astype(F32), axis=0)
    projected = total[0:64]
    inverse = lax.rsqrt((total[64:65] + total[65:66]) / width + 1e-06)
    proj_ref[...] = projected
    inv_ref[...] = inverse
    latent = (inverse * projected).astype(BF)
    noisy_ref[...] = (
        cos_ref[0] * latent.astype(F32) + sin_ref[0] * noise_ref[...].astype(F32)
    ).astype(BF)


def prepare_body(
    place_ref, w_hbm, frames_hbm, hidden_hbm, fold_ref, join_ref, bias_ref, spread_ref,
    w_ref, frames_ref, hidden_ref, sems,
):
    copies = fetch(
        [
            (frames_hbm, frames_ref),
            (hidden_hbm, hidden_ref),
            (w_hbm.at[0, 0], w_ref.at[0]),
            (w_hbm.at[0, 1], w_ref.at[1]),
            (w_hbm.at[0, 2], w_ref.at[2]),
            (w_hbm.at[0, 3], w_ref.at[3]),
        ],
        sems,
    )
    scale = HS ** (-0.5) * math.log2(math.e)
    heads = w_ref.shape[2] // HS
    zero = jnp.zeros((64, HS), BF)
    place = place_ref[0]
    blocks = frames_ref.shape[0]
    copies[0].wait()
    query_frame = frames_ref[pl.ds(place, 1), :]
    ahead = lax.broadcasted_iota(jnp.int32, (128, 128), 0)
    token = lax.broadcasted_iota(jnp.int32, (128, 128), 1)
    for b, offset in enumerate((-2, -1, 0, 1)):
        block = place + offset
        held = jnp.clip(block, 0, blocks - 1)
        key_frame = jnp.broadcast_to(frames_ref[pl.ds(held, 1), :], (128, 128)).T
        key = ahead + offset * 128
        seen = (key_frame <= query_frame) & (token - key < 256)
        seen = seen & (block >= 0) & (block < blocks)
        bias_ref[b * 128 : (b + 1) * 128, :] = jnp.where(seen, 0.0, -1e30)
    copies[1].wait()
    features = hidden_ref.shape[1]
    to = lax.broadcasted_iota(jnp.int32, (192, 320), 0)
    source = lax.broadcasted_iota(jnp.int32, (192, 320), 1)
    turn = (to * 10923) >> 16
    slot = to - turn * 6
    want = turn * 10 + slot
    first = jnp.where((slot < 5) & (source == want), 1.0, 0.0).astype(BF)
    second = jnp.where((slot < 5) & (source == want + 5), 1.0, 0.0).astype(BF)
    for i in range(features // 320):
        piece = hidden_ref[:, i * 320 : (i + 1) * 320]
        rows = slice(i * 192, (i + 1) * 192)
        spread_ref[rows, 0:128] = mm(first, piece, NT).astype(BF)
        spread_ref[rows, 128:256] = mm(second, piece, NT).astype(BF)
    copies[2].wait()
    copies[3].wait()
    for h in range(heads):
        cols = slice(h * HS, (h + 1) * HS)
        fold_ref[h * 64 : (h + 1) * 64, :] = (
            mm(w_ref[1, :, cols], w_ref[0, :, cols], NT) * scale
        ).astype(BF)
    copies[4].wait()
    copies[5].wait()
    for h in range(0, heads, 2):
        one, two = slice(h * HS, (h + 1) * HS), slice((h + 1) * HS, (h + 2) * HS)
        values = jnp.concatenate(
            [
                jnp.concatenate([w_ref[2, :, one], zero], axis=1),
                jnp.concatenate([zero, w_ref[2, :, two]], axis=1),
            ],
            axis=0,
        )
        join_ref[:, h * 64 : (h + 2) * 64] = mm(
            w_ref[3, :, h * HS : (h + 2) * HS], values, NT
        ).astype(BF)


def attend_body(
    role_ref, before2_ref, before1_ref, own_ref, after_ref, fold_ref, join_ref, bias_ref, out_ref,
    query_ref, mixed_ref,
):
    heads = fold_ref.shape[0] // 64
    own = own_ref[...]
    window = jnp.concatenate([before2_ref[...], before1_ref[...], own, after_ref[...]], axis=1)
    row = lax.broadcasted_iota(jnp.int32, (16, 512), 0)
    summing = jnp.concatenate([window, jnp.where(row == 0, 1.0, 0.0).astype(BF)], axis=0)
    keys = window.astype(F32).T.astype(BF)
    query_ref[...] = mm(fold_ref[...], own).astype(BF)
    bias = jnp.concatenate([bias_ref[...]] * GROUP, axis=1)

    def score(h):
        queries = [query_ref[(h + g) * 64 : (h + g + 1) * 64, :] for g in range(GROUP)]
        return mm(keys, jnp.concatenate(queries, axis=1)) + bias

    def soften(scores):
        return jnp.exp2(scores - jnp.max(scores, axis=0, keepdims=True)).astype(BF)

    def mix(h, expo):
        mixed = mm(summing, expo)
        normal = (mixed[0:64] * (1.0 / mixed[64:65])).astype(BF)
        for g in range(GROUP):
            mixed_ref[(h + g) * 64 : (h + g + 1) * 64, :] = normal[:, g * 128 : (g + 1) * 128]

    scores, expo = score(0), None
    for h in range(0, heads + GROUP, GROUP):
        upcoming = score(h + GROUP) if h + GROUP < heads else None
        current = soften(scores) if h < heads else None
        if expo is not None:
            mix(h - GROUP, expo)
        scores, expo = upcoming, current
    predicted = own.astype(F32) + mm(join_ref[...], mixed_ref[...])
    role = role_ref[0]
    weight = jnp.float32(DIFF_TABLE[0])
    for i in range(1, 4):
        weight = jnp.where(role == i, jnp.float32(DIFF_TABLE[i]), weight)
    out_ref[...] = (weight * predicted).astype(BF)


def gap_body(parts_ref, inv_ref, spread_ref, gap_ref, scaled_ref, terms_ref):
    gap = jnp.sum(parts_ref[...].astype(F32), axis=0)
    gap_ref[...] = gap
    scaled = (inv_ref[...] * gap).astype(BF)
    scaled_ref[...] = scaled
    zero = jnp.zeros_like(scaled)
    both = jnp.concatenate(
        [jnp.concatenate([scaled, zero], axis=1), jnp.concatenate([zero, scaled], axis=1)], axis=0
    )
    terms_ref[...] = mm(spread_ref[...], both, NT).astype(BF)


def hidden_grad_body(
    width, gap_ref, proj_ref, inv_ref, scaled_ref, head_ref, gain_ref, hidden_ref, out_ref,
    latent_ref,
):
    inverse = inv_ref[...]
    projected = proj_ref[...]
    latent_ref[...] = (inverse * projected).astype(BF)
    rms_grad = jnp.sum(gap_ref[...] * projected, axis=0, keepdims=True)
    pull = inverse * inverse * inverse * rms_grad / width
    column = jnp.broadcast_to(pull, (128, 128)).T
    gained_grad = mm(scaled_ref[...], head_ref[...], TN)
    for i in range(hidden_ref.shape[1] // 128):
        cols = slice(i * 128, (i + 1) * 128)
        out_ref[:, cols] = (
            gained_grad[:, cols] * gain_ref[i : i + 1, :] - column * hidden_ref[:, cols].astype(F32)
        ).astype(BF)


def finish_body(terms_ref, gain_ref, head_ref, head_grad_ref, gain_grad_ref):
    total = jnp.sum(terms_ref[...].astype(F32), axis=0)
    rows = jnp.concatenate([total[0:5, 0:64], total[0:5, 64:128]], axis=0)
    head_grad_ref[...] = gain_ref[...] * rows
    column = jnp.sum(head_ref[...].astype(F32) * rows, axis=1, keepdims=True)
    column = jnp.concatenate([column, jnp.zeros((118, 1), F32)], axis=0)
    gain_grad_ref[...] = jnp.broadcast_to(column, (128, 128)).T[0:1, 0:10]


def local(hidden, gain, head_weight, noise, timestep, frames, score_weights):
    shape = jax.ShapeDtypeStruct
    tok_rows, features = hidden.shape
    width = features * lax.axis_size("role")
    blocks = lax.axis_size("seq")
    head_t = head_weight.T
    gain_rows = gain.reshape(features // 128, 128)
    place = lax.axis_index("seq").astype(jnp.int32)
    role = lax.axis_index("role").astype(jnp.int32)
    phase = 0.5 * math.pi * timestep.astype(F32) / 1000.0

    sent, noise_t = call(
        project_body, (shape((SENT_ROWS, tok_rows), BF), shape((64, tok_rows), BF)),
        *map(in_hbm, (hidden, gain_rows, head_t, noise.T)), specs=[HBM] * 4, limit=4,
        scratch=[
            pltpu.VMEM(hidden.shape, BF), pltpu.VMEM(gain_rows.shape, F32),
            pltpu.VMEM(head_t.shape, BF), pltpu.SemaphoreType.DMA((3 + features // 256,)),
        ],
    )
    parts = lax.all_gather(sent, "role")
    projected, inverse, noisy = call(
        functools.partial(noisy_body, width),
        (shape((64, tok_rows), F32), shape((1, tok_rows), F32), shape((64, tok_rows), BF)),
        parts, noise_t, jnp.cos(phase), jnp.sin(phase), specs=[VMEM, VMEM, SMEM, SMEM], limit=2,
    )
    near = [from_behind(noisy, "seq", offset) for offset in (2, 1, -1)]
    fold, join, bias, spread = call(
        prepare_body,
        (
            shape((2560, 64), BF), shape((64, 2560), BF), shape((512, 128), F32),
            shape((blocks * 6, 256), BF),
        ),
        place[None], *map(in_hbm, (score_weights, frames.reshape(blocks, tok_rows), hidden)),
        specs=[SMEM] + [HBM] * 3, flops=2_000_000_000, limit=12,
        scratch=[
            pltpu.VMEM(score_weights.shape[1:], BF), pltpu.VMEM((blocks, tok_rows), jnp.int32),
            pltpu.VMEM(hidden.shape, BF), pltpu.SemaphoreType.DMA((6,)),
        ],
    )
    predicted = call(
        attend_body, shape((64, tok_rows), BF),
        role[None], near[0], near[1], noisy, near[2], fold, join, bias,
        specs=[SMEM] + [VMEM] * 7, flops=3_000_000_000, limit=20,
        scratch=[pltpu.VMEM((2560, 128), BF), pltpu.VMEM((2560, 128), BF)],
    )
    gaps = lax.all_gather(predicted, "role")
    gap, scaled, terms = call(
        gap_body,
        (
            shape((64, tok_rows), F32), shape((64, tok_rows), BF),
            shape((blocks * 6, 128), BF),
        ),
        gaps, inverse, spread,
    )
    summed = lax.all_to_all(terms.reshape(blocks, 3, 2, 128), "seq", 0, 0).reshape(blocks, 6, 128)
    hidden_grad, latent = call(
        functools.partial(hidden_grad_body, width), (shape(hidden.shape, BF), shape((64, tok_rows), BF)),
        gap, projected, inverse, scaled, head_t, gain_rows, hidden, flops=1_000_000_000,
    )
    own_gain = lax.dynamic_slice_in_dim(gain, place * 10, 10, 0)
    own_head = lax.dynamic_slice_in_dim(head_weight, place * 10, 10, 0)
    head_grad, gain_grad = call(
        finish_body, (shape((10, 64), F32), shape((1, 10), F32)), summed, own_gain[:, None], own_head
    )
    return (latent.T, hidden_grad, head_grad, gain_grad[0])


def solution(mesh):
    in_specs = (
        P("seq", "role"),
        P("role"),
        P("role", None),
        P("seq", None),
        P(),
        P(),
        P("role", None, None, None),
    )
    out_specs = (P("seq", None), P("seq", "role"), P(("role", "seq"), None), P(("role", "seq")))
    return jax.shard_map(local, mesh=mesh, in_specs=in_specs, out_specs=out_specs, check_vma=False)
```

time: 80.9 us -> 67.3 us (0.83)
  local copies, waits for them, and re-layouts: 7.93 us -> 0.54 us
  Pallas kernels: 14.6 us -> 10.2 us
  other arithmetic: 1.3 us -> 0 us
  starting transfers between devices: 26 us -> 24.8 us
  waiting for transfers between devices: 13 us -> 14 us
    unnamed x19 -> x7, local copies, waits for them, and re-layouts: 6.24 us -> 0.09 us
    pallas_call x7, Pallas kernels: 14.6 us -> 10.2 us  [call(): pl.pallas_call(body, out_shape=outs, in_specs=specs or [VMEM] * len(args)...]
    ppermute x3, waiting for transfers between devices: 0.01 us -> 1.66 us  [from_behind(): return lax.ppermute(block, axis, route)]
    all_to_all x1, starting transfers between devices: 20.5 us -> 19.3 us  [local(): lax.all_to_all(terms.reshape(blocks, 3, 2, 128), 'seq', 0, 0)]
  transfers between devices with their start and end apart: 4 -> 4, of which waited for: 1 -> 2; matrix products, arithmetic and copies ran while one was open for 2% -> 1% of each run, Pallas kernels for 3% -> 5%
where the time goes in v2:
time: 67.3 us; the launch traced here: 67 us
  starting transfers between devices  24.8 us (37%)
  blocking collectives  15.9 us (24%)
  waiting for transfers between devices  14 us (21%)
  Pallas kernels  10.2 us (15%)
  between operations  1.54 us (2%)
    all_to_all x1, starting transfers between devices, local(): lax.all_to_all(terms.reshape(blocks, 3, 2, 128), 'seq', 0, 0)  19.3 us
    all_to_all x1, waiting for transfers between devices, local(): lax.all_to_all(terms.reshape(blocks, 3, 2, 128), 'seq', 0, 0)  12.4 us
    pallas_call x7, Pallas kernels, call(): pl.pallas_call(body, out_shape=outs, in_specs=specs or [VMEM] * len(args)...  10.2 us
    all_gather x1, blocking collectives, local(): parts = lax.all_gather(sent, 'role')  9.16 us
    all_gather x1, blocking collectives, local(): gaps = lax.all_gather(predicted, 'role')  6.75 us
    ppermute x3, starting transfers between devices, from_behind(): return lax.ppermute(block, axis, route)  5.51 us
    ppermute x3, waiting for transfers between devices, from_behind(): return lax.ppermute(block, axis, route)  1.66 us
  transfers between devices with their start and end apart: 4, of which 2 were waited for; matrix products, arithmetic and copies ran while one was open for 1% of the time, Pallas kernels for 5%

profile of v2, /device:TPU:4, one launch (start us, length us, event | category | flops | bytes accessed | tf_op | source)
XLA Modules:
  0.0 67.0 jit_solution(12365542374077055437)
XLA Ops:
  1.4 1.4 %shard_map.102 = (bf16[80,128]{1,0:T(8,128)(2,1)S(1)}, bf16[64,128]{1,0:T(8,128)(2,1)S(1)}) custom-call(bf16[128,1280]{1,0:T(8,128)(2,1)} %hidden_ref.1, f32[10,128]{1,0:T(8,128)} %bitcast.18, bf16[64,1280]{1,0:T(8,128)(2,1)} %bitcast.16, bf16[64,128]{1,0:T(8,128)(2,1)} %bitcast.21), custom_call_target="tpu_custom_call" | custom-call | bytes 513024 | tf_op jit(solution)/shard_map/pallas_call | solution.py:36
  2.9 9.2 %all-gather = bf16[320,128]{1,0:T(8,128)(2,1)S(1)} all-gather(bf16[80,128]{1,0:T(8,128)(2,1)S(1)} %get-tuple-element.20), channel_id=2, replica_groups=mesh['role'=4,'seq'=128] {'role'}, dimensions={0}, use_global_device_ids=true | all-gather | bytes 102400 | tf_op jit(solution)/shard_map/all_gather | solution.py:266
  12.0 1.3 %collective-permute-start = (bf16[64,128]{1,0:T(8,128)(2,1)S(1)}, bf16[64,128]{1,0:T(8,128)(2,1)S(1)}, u32[]{:S(2)}, u32[]{:S(2)}) collective-permute-start(bf16[64,128]{1,0:T(8,128)(2,1)S(1)} %get-tuple-element.22.own_ref), channel_id=1, source_target_pairs={{0,2},{1,3},{2,4},{3,5},{4,6},{5,7},{6,8},{7,9},{8,10},{9,11},{10,... | collective-permute-start | bytes 49160 | tf_op jit(solution)/shard_map/ppermute | solution.py:27
  13.3 2.9 %collective-permute-start.1 = (bf16[64,128]{1,0:T(8,128)(2,1)S(1)}, bf16[64,128]{1,0:T(8,128)(2,1)S(1)}, u32[]{:S(2)}, u32[]{:S(2)}) collective-permute-start(bf16[64,128]{1,0:T(8,128)(2,1)S(1)} %get-tuple-element.22.own_ref), channel_id=1, source_target_pairs={{0,1},{1,2},{2,3},{3,4},{4,5},{5,6},{6,7},{7,8},{8,9},{9,10},{10,1... | collective-permute-start | bytes 49160 | tf_op jit(solution)/shard_map/ppermute | solution.py:27
  16.3 1.3 %collective-permute-start.2 = (bf16[64,128]{1,0:T(8,128)(2,1)S(1)}, bf16[64,128]{1,0:T(8,128)(2,1)S(1)}, u32[]{:S(2)}, u32[]{:S(2)}) collective-permute-start(bf16[64,128]{1,0:T(8,128)(2,1)S(1)} %get-tuple-element.22.own_ref), channel_id=1, source_target_pairs={{1,0},{2,1},{3,2},{4,3},{5,4},{6,5},{7,6},{8,7},{9,8},{10,9},{11,1... | collective-permute-start | bytes 49160 | tf_op jit(solution)/shard_map/ppermute | solution.py:27
  17.6 2.6 %shard_map.104 = (bf16[2560,64]{1,0:T(8,128)(2,1)S(1)}, bf16[64,2560]{1,0:T(8,128)(2,1)S(1)}, f32[512,128]{1,0:T(8,128)S(1)}, bf16[768,256]{1,0:T(8,128)(2,1)S(1)}) custom-call(s32[1]{0:T(128)} %bitcast.5.place_ref, bf16[1,4,64,5120]{3,2,1,0:T(8,128)(2,1)} %w_hbm.1, s32[128,128]{1,0:T(8,128)} %bitcast.22, bf16[128,1280]{1,0:T(8,128)(2,1)} %hidden_ref.1), custom_call_target="tpu_custom_call" | custom-call | flops 2000000000 | bytes 3014660 | tf_op jit(solution)/shard_map/pallas_call | solution.py:36
  20.2 0.0 collective-permute-done.before2_ref
  20.2 0.0 collective-permute-done.1.before1_ref
  20.3 1.7 %collective-permute-done.2.after_ref = bf16[64,128]{1,0:T(8,128)(2,1)S(1)} collective-permute-done((bf16[64,128]{1,0:T(8,128)(2,1)S(1)}, bf16[64,128]{1,0:T(8,128)(2,1)S(1)}, u32[]{:S(2)}, u32[]{:S(2)}) %collective-permute-start.2) | collective-permute-done | bytes 16416 | tf_op jit(solution)/shard_map/ppermute | solution.py:27
  21.9 0.0 copy-start.1
  21.9 0.0 copy-start.2
  21.9 0.0 copy-start
  21.9 3.2 %shard_map.105 = bf16[64,128]{1,0:T(8,128)(2,1)S(1)} custom-call(s32[1]{0:T(128)} %bitcast.role_ref, bf16[64,128]{1,0:T(8,128)(2,1)S(1)} %collective-permute-done.before2_ref, bf16[64,128]{1,0:T(8,128)(2,1)S(1)} %collective-permute-done.1.before1_ref, bf16[64,128]{1,0:T(8,128)(2,1)S(1)} %get-tuple-element.22.own_ref, ...), custom_call_target="tpu_custom_call" | custom-call | flops 3000000000 | bytes 983044 | tf_op jit(solution)/shard_map/pallas_call | solution.py:36
  25.1 6.8 %all-gather.1 = bf16[256,128]{1,0:T(8,128)(2,1)S(1)} all-gather(bf16[64,128]{1,0:T(8,128)(2,1)S(1)} %shard_map.105), channel_id=3, replica_groups=mesh['role'=4,'seq'=128] {'role'}, dimensions={0}, use_global_device_ids=true | all-gather | bytes 81920 | tf_op jit(solution)/shard_map/all_gather | solution.py:292
  31.8 0.9 %shard_map.106 = (f32[64,128]{1,0:T(8,128)S(1)}, bf16[64,128]{1,0:T(8,128)(2,1)S(1)}, bf16[768,128]{1,0:T(8,128)(2,1)}) custom-call(bf16[4,64,128]{2,1,0:T(8,128)(2,1)S(1)} %bitcast.15, f32[1,128]{1,0:T(1,128)S(1)} %get-tuple-element.26.inv_ref, bf16[768,256]{1,0:T(8,128)(2,1)S(1)} %get-tuple-element.27.spread_ref), custom_call_target="tpu_custom_call" | custom-call | bytes 459264 | tf_op jit(solution)/shard_map/pallas_call | solution.py:36
  32.8 19.3 %all-to-all-start = ((bf16[128,3,2,128]{3,2,1,0:T(2,128)(2,1)}), bf16[128,3,2,128]{3,2,1,0:T(2,128)(2,1)S(1)}, u32[]{:S(2)}, u32[]{:S(2)}) async-start(bf16[128,3,2,128]{3,2,1,0:T(2,128)(2,1)} %bitcast.9), calls=%async_computation | async-start | bytes 393216 | tf_op jit(solution)/shard_map/all_to_all | solution.py:301
  52.1 0.0 copy-done.1
  52.1 0.1 constant_dynamic-slice_fusion
  52.2 0.1 copy.21.head_ref
  52.3 0.0 copy-done.2
  52.3 0.1 dynamic-slice_bitcast_fusion
  52.4 0.1 copy.20.gain_ref
  52.5 0.0 copy-done
  52.5 1.0 %shard_map.107 = (bf16[128,1280]{1,0:T(8,128)(2,1)}, bf16[64,128]{1,0:T(8,128)(2,1)}) custom-call(f32[64,128]{1,0:T(8,128)S(1)} %get-tuple-element.28.gap_ref, f32[64,128]{1,0:T(8,128)S(1)} %get-tuple-element.29.proj_ref, f32[1,128]{1,0:T(1,128)S(1)} %get-tuple-element.26.inv_ref, bf16[64,128]{1,0:T(8,128)(2,1)S(1)} %get-tuple-element.30.scaled_ref, ...), custom_call_target="tpu_custom_call" | custom-call | flops 1000000000 | bytes 579072 | tf_op jit(solution)/shard_map/pallas_call | solution.py:36
  53.5 12.4 %all-to-all-done = bf16[128,3,2,128]{3,2,1,0:T(2,128)(2,1)S(1)} async-done(((bf16[128,3,2,128]{3,2,1,0:T(2,128)(2,1)}), bf16[128,3,2,128]{3,2,1,0:T(2,128)(2,1)S(1)}, u32[]{:S(2)}, u32[]{:S(2)}) %all-to-all-start) | async-done | bytes 196640 | tf_op jit(solution)/shard_map/all_to_all | solution.py:301
  65.9 0.1 copy.19.terms_ref
  66.1 1.0 %shard_map.108 = (f32[10,64]{1,0:T(8,128)}, f32[1,10]{1,0:T(1,128)}) custom-call(bf16[128,6,128]{2,1,0:T(8,128)(2,1)S(1)} %copy.19.terms_ref, f32[10,1]{1,0:T(8,128)S(1)} %copy.20.gain_ref, bf16[10,64]{1,0:T(8,128)(2,1)S(1)} %copy.21.head_ref), custom_call_target="tpu_custom_call" | custom-call | bytes 197928 | tf_op jit(solution)/shard_map/pallas_call | solution.py:36
  (2 shorter events, 0.1 us)
Async XLA Ops:
  12.0 8.2 %collective-permute-start = (bf16[64,128]{1,0:T(8,128)(2,1)S(1)}, bf16[64,128]{1,0:T(8,128)(2,1)S(1)}, u32[]{:S(2)}, u32[]{:S(2)}) collective-permute-start(bf16[64,128]{1,0:T(8,128)(2,1)S(1)} %get-tuple-element.22.own_ref), channel_id=1, source_target_pairs={{0,2},{1,3},{2,4},{3,5},{4,6},{5,7},{6,8},{7,9},{8,10},{9,11},{10,... | collective-permute-start | bytes 49160 | tf_op jit(solution)/shard_map/ppermute | solution.py:27
  13.3 6.9 %collective-permute-start.1 = (bf16[64,128]{1,0:T(8,128)(2,1)S(1)}, bf16[64,128]{1,0:T(8,128)(2,1)S(1)}, u32[]{:S(2)}, u32[]{:S(2)}) collective-permute-start(bf16[64,128]{1,0:T(8,128)(2,1)S(1)} %get-tuple-element.22.own_ref), channel_id=1, source_target_pairs={{0,1},{1,2},{2,3},{3,4},{4,5},{5,6},{6,7},{7,8},{8,9},{9,10},{10,1... | collective-permute-start | bytes 49160 | tf_op jit(solution)/shard_map/ppermute | solution.py:27
  16.3 5.6 %collective-permute-start.2 = (bf16[64,128]{1,0:T(8,128)(2,1)S(1)}, bf16[64,128]{1,0:T(8,128)(2,1)S(1)}, u32[]{:S(2)}, u32[]{:S(2)}) collective-permute-start(bf16[64,128]{1,0:T(8,128)(2,1)S(1)} %get-tuple-element.22.own_ref), channel_id=1, source_target_pairs={{1,0},{2,1},{3,2},{4,3},{5,4},{6,5},{7,6},{8,7},{9,8},{10,9},{11,1... | collective-permute-start | bytes 49160 | tf_op jit(solution)/shard_map/ppermute | solution.py:27
  21.9 30.2 %copy-start.1 = (bf16[1280,64]{0,1:T(8,128)(2,1)S(1)}, bf16[1280,64]{0,1:T(8,128)(2,1)}, u32[]{:S(2)}) copy-start(bf16[1280,64]{0,1:T(8,128)(2,1)} %param.9) | copy-start | bytes 491524
  21.9 30.4 %copy-start.2 = (f32[1280]{0:T(1024)S(1)}, f32[1280]{0:T(1024)}, u32[]{:S(2)}) copy-start(f32[1280]{0:T(1024)} %param.8) | copy-start | bytes 15364
  21.9 30.6 %copy-start = (bf16[128,1280]{1,0:T(8,128)(2,1)S(1)}, bf16[128,1280]{1,0:T(8,128)(2,1)}, u32[]{:S(2)}) copy-start(bf16[128,1280]{1,0:T(8,128)(2,1)} %hidden_ref.1) | copy-start | bytes 983044
  32.8 33.1 %all-to-all-start = ((bf16[128,3,2,128]{3,2,1,0:T(2,128)(2,1)}), bf16[128,3,2,128]{3,2,1,0:T(2,128)(2,1)S(1)}, u32[]{:S(2)}, u32[]{:S(2)}) async-start(bf16[128,3,2,128]{3,2,1,0:T(2,128)(2,1)} %bitcast.9), calls=%async_computation | async-start | bytes 393216 | tf_op jit(solution)/shard_map/all_to_all | solution.py:301

commit v3 on v2

--- a/solution.py
+++ b/solution.py
@@ -17,14 +17,20 @@
 TN = (((0,), (0,)), ((), ()))
 SENT_ROWS = 80
 GROUP = 4
+JOIN_FROM = 20
 VMEM, SMEM = pl.BlockSpec(memory_space=pltpu.VMEM), pl.BlockSpec(memory_space=pltpu.SMEM)
 HBM = pl.BlockSpec(memory_space=pltpu.HBM)
 
 
-def from_behind(block, axis, distance):
-    devices = range(lax.axis_size(axis))
-    route = [(i - distance, i) for i in devices if i - distance in devices]
-    return lax.ppermute(block, axis, route)
+def move(block, target):
+    roles, places = lax.axis_size("role"), lax.axis_size("seq")
+    route = []
+    for r in range(roles):
+        for s in range(places):
+            to_role, to_place = target(r, s)
+            if 0 <= to_place < places:
+                route.append((r * places + s, to_role * places + to_place))
+    return lax.ppermute(block, ("role", "seq"), route)
 
 
 def mm(a, b, dims=NN):
@@ -55,15 +61,16 @@
 
 
 def project_body(
-    hidden_hbm, gain_hbm, head_hbm, noise_hbm, out_ref, noise_ref, hidden_ref, gain_ref, head_ref,
-    sems,
+    hidden_hbm, gain_hbm, head_hbm, noise_hbm, frames_hbm, w_hbm, out_ref, noise_ref, hidden_ref,
+    frames_ref, w_ref, gain_ref, head_ref, sems,
 ):
     features = hidden_ref.shape[1]
     pieces = [slice(i, i + 256) for i in range(0, features, 256)]
     copies = fetch(
         [(gain_hbm, gain_ref)]
         + [(hidden_hbm.at[:, piece], hidden_ref.at[:, piece]) for piece in pieces]
-        + [(head_hbm, head_ref), (noise_hbm, noise_ref)],
+        + [(head_hbm, head_ref), (noise_hbm, noise_ref), (frames_hbm, frames_ref)]
+        + [(w_hbm.at[0, i], w_ref.at[i]) for i in range(2)],
         sems,
     )
     copies[0].wait()
@@ -74,13 +81,14 @@
         hidden = hidden_ref[:, i * 128 : (i + 1) * 128].astype(F32)
         gained.append((hidden * gain_ref[i : i + 1, :]).astype(BF))
         lanes = lanes + hidden * hidden
-    copies[-2].wait()
+    copies[1 + len(pieces)].wait()
     out_ref[0:64, :] = mm(head_ref[...], jnp.concatenate(gained, axis=1), NT).astype(BF)
     total = jnp.sum(lanes.T, axis=0, keepdims=True)
     high = total.astype(BF).astype(F32)
     row = lax.broadcasted_iota(jnp.int32, (16, 128), 0)
     out_ref[64:80, :] = jnp.where(row == 0, high, jnp.where(row == 1, total - high, 0.0)).astype(BF)
-    copies[-1].wait()
+    for copy in copies[2 + len(pieces) :]:
+        copy.wait()
 
 
 def noisy_body(width, parts_ref, noise_ref, cos_ref, sin_ref, proj_ref, inv_ref, noisy_ref):
@@ -95,27 +103,11 @@
     ).astype(BF)
 
 
-def prepare_body(
-    place_ref, w_hbm, frames_hbm, hidden_hbm, fold_ref, join_ref, bias_ref, spread_ref,
-    w_ref, frames_ref, hidden_ref, sems,
-):
-    copies = fetch(
-        [
-            (frames_hbm, frames_ref),
-            (hidden_hbm, hidden_ref),
-            (w_hbm.at[0, 0], w_ref.at[0]),
-            (w_hbm.at[0, 1], w_ref.at[1]),
-            (w_hbm.at[0, 2], w_ref.at[2]),
-            (w_hbm.at[0, 3], w_ref.at[3]),
-        ],
-        sems,
-    )
+def prepare_body(place_ref, w_ref, frames_ref, hidden_ref, fold_ref, bias_ref, spread_ref):
     scale = HS ** (-0.5) * math.log2(math.e)
     heads = w_ref.shape[2] // HS
-    zero = jnp.zeros((64, HS), BF)
     place = place_ref[0]
     blocks = frames_ref.shape[0]
-    copies[0].wait()
     query_frame = frames_ref[pl.ds(place, 1), :]
     ahead = lax.broadcasted_iota(jnp.int32, (128, 128), 0)
     token = lax.broadcasted_iota(jnp.int32, (128, 128), 1)
@@ -127,7 +119,6 @@
         seen = (key_frame <= query_frame) & (token - key < 256)
         seen = seen & (block >= 0) & (block < blocks)
         bias_ref[b * 128 : (b + 1) * 128, :] = jnp.where(seen, 0.0, -1e30)
-    copies[1].wait()
     features = hidden_ref.shape[1]
     to = lax.broadcasted_iota(jnp.int32, (192, 320), 0)
     source = lax.broadcasted_iota(jnp.int32, (192, 320), 1)
@@ -141,41 +132,34 @@
         rows = slice(i * 192, (i + 1) * 192)
         spread_ref[rows, 0:128] = mm(first, piece, NT).astype(BF)
         spread_ref[rows, 128:256] = mm(second, piece, NT).astype(BF)
-    copies[2].wait()
-    copies[3].wait()
     for h in range(heads):
         cols = slice(h * HS, (h + 1) * HS)
         fold_ref[h * 64 : (h + 1) * 64, :] = (
             mm(w_ref[1, :, cols], w_ref[0, :, cols], NT) * scale
         ).astype(BF)
-    copies[4].wait()
-    copies[5].wait()
-    for h in range(0, heads, 2):
-        one, two = slice(h * HS, (h + 1) * HS), slice((h + 1) * HS, (h + 2) * HS)
-        values = jnp.concatenate(
-            [
-                jnp.concatenate([w_ref[2, :, one], zero], axis=1),
-                jnp.concatenate([zero, w_ref[2, :, two]], axis=1),
-            ],
-            axis=0,
-        )
-        join_ref[:, h * 64 : (h + 2) * 64] = mm(
-            w_ref[3, :, h * HS : (h + 2) * HS], values, NT
-        ).astype(BF)
 
 
 def attend_body(
-    role_ref, before2_ref, before1_ref, own_ref, after_ref, fold_ref, join_ref, bias_ref, out_ref,
-    query_ref, mixed_ref,
+    role_ref, before1_ref, fetched_ref, swapped_ref, own_ref, fold_ref, bias_ref, w_hbm, out_ref,
+    query_ref, mixed_ref, join_ref, w_ref, sems,
 ):
+    values_copy, output_copy = fetch(
+        [(w_hbm.at[0, 2], w_ref.at[0]), (w_hbm.at[0, 3], w_ref.at[1])], sems
+    )
     heads = fold_ref.shape[0] // 64
+    role = role_ref[0]
     own = own_ref[...]
-    window = jnp.concatenate([before2_ref[...], before1_ref[...], own, after_ref[...]], axis=1)
+    fetched, swapped = fetched_ref[...], swapped_ref[...]
+    first_core = role % 2 == 0
+    before2 = jnp.where(first_core, fetched, swapped)
+    after = jnp.where(first_core, swapped, fetched)
+    window = jnp.concatenate([before2, before1_ref[...], own, after], axis=1)
     row = lax.broadcasted_iota(jnp.int32, (16, 512), 0)
     summing = jnp.concatenate([window, jnp.where(row == 0, 1.0, 0.0).astype(BF)], axis=0)
     keys = window.astype(F32).T.astype(BF)
     query_ref[...] = mm(fold_ref[...], own).astype(BF)
     bias = jnp.concatenate([bias_ref[...]] * GROUP, axis=1)
+    zero = jnp.zeros((64, HS), BF)
 
     def score(h):
         queries = [query_ref[(h + g) * 64 : (h + g + 1) * 64, :] for g in range(GROUP)]
@@ -190,15 +174,34 @@
         for g in range(GROUP):
             mixed_ref[(h + g) * 64 : (h + g + 1) * 64, :] = normal[:, g * 128 : (g + 1) * 128]
 
+    def join(h):
+        one, two = slice(h * HS, (h + 1) * HS), slice((h + 1) * HS, (h + 2) * HS)
+        values = jnp.concatenate(
+            [
+                jnp.concatenate([w_ref[0, :, one], zero], axis=1),
+                jnp.concatenate([zero, w_ref[0, :, two]], axis=1),
+            ],
+            axis=0,
+        )
+        join_ref[:, h * 64 : (h + 2) * 64] = mm(
+            w_ref[1, :, h * HS : (h + 2) * HS], values, NT
+        ).astype(BF)
+
+    pairs = list(range(0, heads, 2))
     scores, expo = score(0), None
     for h in range(0, heads + GROUP, GROUP):
         upcoming = score(h + GROUP) if h + GROUP < heads else None
         current = soften(scores) if h < heads else None
         if expo is not None:
             mix(h - GROUP, expo)
+        if h == JOIN_FROM:
+            values_copy.wait()
+            output_copy.wait()
+        if h >= JOIN_FROM:
+            for _ in range(-(-len(pairs) * GROUP // (heads + GROUP - h))):
+                join(pairs.pop(0))
         scores, expo = upcoming, current
     predicted = own.astype(F32) + mm(join_ref[...], mixed_ref[...])
-    role = role_ref[0]
     weight = jnp.float32(DIFF_TABLE[0])
     for i in range(1, 4):
         weight = jnp.where(role == i, jnp.float32(DIFF_TABLE[i]), weight)
@@ -255,12 +258,24 @@
     role = lax.axis_index("role").astype(jnp.int32)
     phase = 0.5 * math.pi * timestep.astype(F32) / 1000.0
 
-    sent, noise_t = call(
-        project_body, (shape((SENT_ROWS, tok_rows), BF), shape((64, tok_rows), BF)),
-        *map(in_hbm, (hidden, gain_rows, head_t, noise.T)), specs=[HBM] * 4, limit=4,
+    wide = score_weights.shape[2:]
+    sent, noise_t, hidden_v, frames_v, query_key = call(
+        project_body,
+        (
+            shape((SENT_ROWS, tok_rows), BF), shape((64, tok_rows), BF), shape(hidden.shape, BF),
+            shape((blocks, tok_rows), jnp.int32), shape((2, *wide), BF),
+        ),
+        *map(
+            in_hbm,
+            (
+                hidden, gain_rows, head_t, noise.T, frames.reshape(blocks, tok_rows),
+                score_weights,
+            ),
+        ),
+        specs=[HBM] * 6,
         scratch=[
-            pltpu.VMEM(hidden.shape, BF), pltpu.VMEM(gain_rows.shape, F32),
-            pltpu.VMEM(head_t.shape, BF), pltpu.SemaphoreType.DMA((3 + features // 256,)),
+            pltpu.VMEM(gain_rows.shape, F32), pltpu.VMEM(head_t.shape, BF),
+            pltpu.SemaphoreType.DMA((6 + features // 256,)),
         ],
     )
     parts = lax.all_gather(sent, "role")
@@ -269,25 +284,23 @@
         (shape((64, tok_rows), F32), shape((1, tok_rows), F32), shape((64, tok_rows), BF)),
         parts, noise_t, jnp.cos(phase), jnp.sin(phase), specs=[VMEM, VMEM, SMEM, SMEM], limit=2,
     )
-    near = [from_behind(noisy, "seq", offset) for offset in (2, 1, -1)]
-    fold, join, bias, spread = call(
+    fetched = move(noisy, lambda r, s: (r, s + 2 if r % 2 == 0 else s - 1))
+    before1 = move(noisy, lambda r, s: (r, s + 1))
+    swapped = move(fetched, lambda r, s: (r ^ 1, s))
+    fold, bias, spread = call(
         prepare_body,
-        (
-            shape((2560, 64), BF), shape((64, 2560), BF), shape((512, 128), F32),
-            shape((blocks * 6, 256), BF),
-        ),
-        place[None], *map(in_hbm, (score_weights, frames.reshape(blocks, tok_rows), hidden)),
-        specs=[SMEM] + [HBM] * 3, flops=2_000_000_000, limit=12,
-        scratch=[
-            pltpu.VMEM(score_weights.shape[1:], BF), pltpu.VMEM((blocks, tok_rows), jnp.int32),
-            pltpu.VMEM(hidden.shape, BF), pltpu.SemaphoreType.DMA((6,)),
-        ],
+        (shape((2560, 64), BF), shape((512, 128), F32), shape((blocks * 6, 256), BF)),
+        place[None], query_key, frames_v, hidden_v, specs=[SMEM] + [VMEM] * 3,
+        flops=2_000_000_000,
     )
     predicted = call(
         attend_body, shape((64, tok_rows), BF),
-        role[None], near[0], near[1], noisy, near[2], fold, join, bias,
-        specs=[SMEM] + [VMEM] * 7, flops=3_000_000_000, limit=20,
-        scratch=[pltpu.VMEM((2560, 128), BF), pltpu.VMEM((2560, 128), BF)],
+        role[None], before1, fetched, swapped, noisy, fold, bias, in_hbm(score_weights),
+        specs=[SMEM] + [VMEM] * 6 + [HBM], flops=3_000_000_000, limit=24,
+        scratch=[
+            pltpu.VMEM((2560, 128), BF), pltpu.VMEM((2560, 128), BF), pltpu.VMEM((64, 2560), BF),
+            pltpu.VMEM((2, *wide), BF), pltpu.SemaphoreType.DMA((2,)),
+        ],
     )
     gaps = lax.all_gather(predicted, "role")
     gap, scaled, terms = call(
@@ -301,7 +314,7 @@
     summed = lax.all_to_all(terms.reshape(blocks, 3, 2, 128), "seq", 0, 0).reshape(blocks, 6, 128)
     hidden_grad, latent = call(
         functools.partial(hidden_grad_body, width), (shape(hidden.shape, BF), shape((64, tok_rows), BF)),
-        gap, projected, inverse, scaled, head_t, gain_rows, hidden, flops=1_000_000_000,
+        gap, projected, inverse, scaled, head_t, gain_rows, hidden_v, flops=1_000_000_000,
     )
     own_gain = lax.dynamic_slice_in_dim(gain, place * 10, 10, 0)
     own_head = lax.dynamic_slice_in_dim(head_weight, place * 10, 10, 0)

time: 67.3 us -> 64.9 us (0.964)
  waiting for transfers between devices: 14 us -> 12.4 us
  Pallas kernels: 10.2 us -> 9.19 us
    all_to_all x1, starting transfers between devices: 19.3 us -> 17.3 us  [local(): lax.all_to_all(terms.reshape(blocks, 3, 2, 128), 'seq', 0, 0)]
    ppermute x3, starting transfers between devices: 5.51 us -> 7.53 us  [move(): return lax.ppermute(block, ('role', 'seq'), route)]
    ppermute x3, waiting for transfers between devices: 1.66 us -> 0.01 us  [move(): return lax.ppermute(block, ('role', 'seq'), route)]
    pallas_call x7, Pallas kernels: 10.2 us -> 9.19 us  [call(): pl.pallas_call(body, out_shape=outs, in_specs=specs or [VMEM] * len(args)...]
  transfers between devices with their start and end apart: 4 -> 4, of which waited for: 2 -> 1; matrix products, arithmetic and copies ran while one was open for 1% -> 1% of each run, Pallas kernels for 5% -> 3%
where the time goes in v3:
time: 64.9 us; the launch traced here: 64.6 us
  starting transfers between devices  24.8 us (38%)
  blocking collectives  16.1 us (25%)
  waiting for transfers between devices  12.4 us (19%)
  Pallas kernels  9.19 us (14%)
  between operations  1.56 us (2%)
    all_to_all x1, starting transfers between devices, local(): lax.all_to_all(terms.reshape(blocks, 3, 2, 128), 'seq', 0, 0)  17.3 us
    all_to_all x1, waiting for transfers between devices, local(): lax.all_to_all(terms.reshape(blocks, 3, 2, 128), 'seq', 0, 0)  12.4 us
    pallas_call x7, Pallas kernels, call(): pl.pallas_call(body, out_shape=outs, in_specs=specs or [VMEM] * len(args)...  9.19 us
    all_gather x1, blocking collectives, local(): parts = lax.all_gather(sent, 'role')  9.16 us
    ppermute x3, starting transfers between devices, move(): return lax.ppermute(block, ('role', 'seq'), route)  7.53 us
    all_gather x1, blocking collectives, local(): gaps = lax.all_gather(predicted, 'role')  6.96 us
  transfers between devices with their start and end apart: 4, of which 1 were waited for; matrix products, arithmetic and copies ran while one was open for 1% of the time, Pallas kernels for 3%

profile of v3, /device:TPU:4, one launch (start us, length us, event | category | flops | bytes accessed | tf_op | source)
XLA Modules:
  0.0 64.6 jit_solution(10886596396137731232)
XLA Ops:
  1.4 1.7 %shard_map.102 = (bf16[80,128]{1,0:T(8,128)(2,1)S(1)}, bf16[64,128]{1,0:T(8,128)(2,1)S(1)}, bf16[128,1280]{1,0:T(8,128)(2,1)S(1)}, s32[128,128]{1,0:T(8,128)S(1)}, bf16[2,64,5120]{2,1,0:T(8,128)(2,1)S(1)}) custom-call(bf16[128,1280]{1,0:T(8,128)(2,1)} %hidden_hbm.1, f32[10,128]{1,0:T(8,128)} %bitcast.18, bf16[64,1280]{1,0:T(8,128)(2,1)} %bitcast.16, ...), custom_call_target="tpu_custom_call" | custom-call | bytes 3200000 | tf_op jit(solution)/shard_map/pallas_call | solution.py:42
  3.1 9.2 %all-gather = bf16[320,128]{1,0:T(8,128)(2,1)S(1)} all-gather(bf16[80,128]{1,0:T(8,128)(2,1)S(1)} %get-tuple-element.22), channel_id=2, replica_groups=mesh['role'=4,'seq'=128] {'role'}, dimensions={0}, use_global_device_ids=true | all-gather | bytes 102400 | tf_op jit(solution)/shard_map/all_gather | solution.py:281
  12.3 1.3 %collective-permute-start.1 = (bf16[64,128]{1,0:T(8,128)(2,1)S(1)}, bf16[64,128]{1,0:T(8,128)(2,1)S(1)}, u32[]{:S(2)}, u32[]{:S(2)}) collective-permute-start(bf16[64,128]{1,0:T(8,128)(2,1)S(1)} %get-tuple-element.24.own_ref), channel_id=1, source_target_pairs={{0,2},{1,3},{2,4},{3,5},{4,6},{5,7},{6,8},{7,9},{8,10},{9,11},{10,... | collective-permute-start | bytes 49160 | tf_op jit(solution)/shard_map/ppermute | solution.py:33
  13.6 2.9 %collective-permute-start = (bf16[64,128]{1,0:T(8,128)(2,1)S(1)}, bf16[64,128]{1,0:T(8,128)(2,1)S(1)}, u32[]{:S(2)}, u32[]{:S(2)}) collective-permute-start(bf16[64,128]{1,0:T(8,128)(2,1)S(1)} %get-tuple-element.24.own_ref), channel_id=1, source_target_pairs={{0,1},{1,2},{2,3},{3,4},{4,5},{5,6},{6,7},{7,8},{8,9},{9,10},{10,1... | collective-permute-start | bytes 49160 | tf_op jit(solution)/shard_map/ppermute | solution.py:33
  16.6 0.0 collective-permute-done.1.fetched_ref
  16.6 3.3 %collective-permute-start.2 = (bf16[64,128]{1,0:T(8,128)(2,1)S(1)}, bf16[64,128]{1,0:T(8,128)(2,1)S(1)}, u32[]{:S(2)}, u32[]{:S(2)}) collective-permute-start(bf16[64,128]{1,0:T(8,128)(2,1)S(1)} %collective-permute-done.1.fetched_ref), channel_id=1, source_target_pairs={{0,128},{1,129},{2,130},{3,131},{4,132},{5,133},{6,134},{7,135},{8... | collective-permute-start | bytes 49160 | tf_op jit(solution)/shard_map/ppermute | solution.py:33
  19.9 0.9 %shard_map.104 = (bf16[2560,64]{1,0:T(8,128)(2,1)S(1)}, f32[512,128]{1,0:T(8,128)S(1)}, bf16[768,256]{1,0:T(8,128)(2,1)S(1)}) custom-call(s32[1]{0:T(128)} %bitcast.6.place_ref, bf16[2,64,5120]{2,1,0:T(8,128)(2,1)S(1)} %get-tuple-element.25.w_ref, s32[128,128]{1,0:T(8,128)S(1)} %get-tuple-element.26.frames_ref, ...), custom_call_target="tpu_custom_call" | custom-call | flops 2000000000 | bytes 1703940 | tf_op jit(solution)/shard_map/pallas_call | solution.py:42
  20.8 0.0 collective-permute-done.before1_ref
  20.8 0.0 collective-permute-done.2.swapped_ref
  20.8 0.0 copy-start
  20.8 0.0 copy-start.1
  20.8 3.7 %shard_map.105 = bf16[64,128]{1,0:T(8,128)(2,1)S(1)} custom-call(s32[1]{0:T(128)} %bitcast.role_ref, bf16[64,128]{1,0:T(8,128)(2,1)S(1)} %collective-permute-done.before1_ref, bf16[64,128]{1,0:T(8,128)(2,1)S(1)} %collective-permute-done.1.fetched_ref, bf16[64,128]{1,0:T(8,128)(2,1)S(1)} %collective-permute-done.2.swapped_ref, ...), custom_call_target="tpu_custom_call" | custom-call | flops 3000000000 | bytes 3276804 | tf_op jit(solution)/shard_map/pallas_call | solution.py:42
  24.5 7.0 %all-gather.1 = bf16[256,128]{1,0:T(8,128)(2,1)S(1)} all-gather(bf16[64,128]{1,0:T(8,128)(2,1)S(1)} %shard_map.105), channel_id=3, replica_groups=mesh['role'=4,'seq'=128] {'role'}, dimensions={0}, use_global_device_ids=true | all-gather | bytes 81920 | tf_op jit(solution)/shard_map/all_gather | solution.py:305
  31.4 0.9 %shard_map.106 = (f32[64,128]{1,0:T(8,128)S(1)}, bf16[64,128]{1,0:T(8,128)(2,1)S(1)}, bf16[768,128]{1,0:T(8,128)(2,1)}) custom-call(bf16[4,64,128]{2,1,0:T(8,128)(2,1)S(1)} %bitcast.15, f32[1,128]{1,0:T(1,128)S(1)} %get-tuple-element.30.inv_ref, bf16[768,256]{1,0:T(8,128)(2,1)S(1)} %get-tuple-element.31.spread_ref), custom_call_target="tpu_custom_call" | custom-call | bytes 459264 | tf_op jit(solution)/shard_map/pallas_call | solution.py:42
  32.4 17.3 %all-to-all-start = ((bf16[128,3,2,128]{3,2,1,0:T(2,128)(2,1)}), bf16[128,3,2,128]{3,2,1,0:T(2,128)(2,1)S(1)}, u32[]{:S(2)}, u32[]{:S(2)}) async-start(bf16[128,3,2,128]{3,2,1,0:T(2,128)(2,1)} %bitcast.9), calls=%async_computation | async-start | bytes 393216 | tf_op jit(solution)/shard_map/all_to_all | solution.py:314
  49.7 0.0 copy-done
  49.7 0.1 constant_dynamic-slice_fusion
  49.8 0.1 copy.21.head_ref
  49.9 0.0 copy-done.1
  49.9 0.1 dynamic-slice_bitcast_fusion
  50.0 0.1 copy.20.gain_ref
  50.1 1.0 %shard_map.107 = (bf16[128,1280]{1,0:T(8,128)(2,1)}, bf16[64,128]{1,0:T(8,128)(2,1)}) custom-call(f32[64,128]{1,0:T(8,128)S(1)} %get-tuple-element.32.gap_ref, f32[64,128]{1,0:T(8,128)S(1)} %get-tuple-element.33.proj_ref, f32[1,128]{1,0:T(1,128)S(1)} %get-tuple-element.30.inv_ref, bf16[64,128]{1,0:T(8,128)(2,1)S(1)} %get-tuple-element.34.scaled_ref, ...), custom_call_target="tpu_custom_call" | custom-call | flops 1000000000 | bytes 579072 | tf_op jit(solution)/shard_map/pallas_call | solution.py:42
  51.1 12.4 %all-to-all-done = bf16[128,3,2,128]{3,2,1,0:T(2,128)(2,1)S(1)} async-done(((bf16[128,3,2,128]{3,2,1,0:T(2,128)(2,1)}), bf16[128,3,2,128]{3,2,1,0:T(2,128)(2,1)S(1)}, u32[]{:S(2)}, u32[]{:S(2)}) %all-to-all-start) | async-done | bytes 196640 | tf_op jit(solution)/shard_map/all_to_all | solution.py:314
  63.5 0.1 copy.19.terms_ref
  63.7 1.0 %shard_map.108 = (f32[10,64]{1,0:T(8,128)}, f32[1,10]{1,0:T(1,128)}) custom-call(bf16[128,6,128]{2,1,0:T(8,128)(2,1)S(1)} %copy.19.terms_ref, f32[10,1]{1,0:T(8,128)S(1)} %copy.20.gain_ref, bf16[10,64]{1,0:T(8,128)(2,1)S(1)} %copy.21.head_ref), custom_call_target="tpu_custom_call" | custom-call | bytes 197928 | tf_op jit(solution)/shard_map/pallas_call | solution.py:42
  (2 shorter events, 0.1 us)
Async XLA Ops:
  12.3 4.2 %collective-permute-start.1 = (bf16[64,128]{1,0:T(8,128)(2,1)S(1)}, bf16[64,128]{1,0:T(8,128)(2,1)S(1)}, u32[]{:S(2)}, u32[]{:S(2)}) collective-permute-start(bf16[64,128]{1,0:T(8,128)(2,1)S(1)} %get-tuple-element.24.own_ref), channel_id=1, source_target_pairs={{0,2},{1,3},{2,4},{3,5},{4,6},{5,7},{6,8},{7,9},{8,10},{9,11},{10,... | collective-permute-start | bytes 49160 | tf_op jit(solution)/shard_map/ppermute | solution.py:33
  13.6 7.1 %collective-permute-start = (bf16[64,128]{1,0:T(8,128)(2,1)S(1)}, bf16[64,128]{1,0:T(8,128)(2,1)S(1)}, u32[]{:S(2)}, u32[]{:S(2)}) collective-permute-start(bf16[64,128]{1,0:T(8,128)(2,1)S(1)} %get-tuple-element.24.own_ref), channel_id=1, source_target_pairs={{0,1},{1,2},{2,3},{3,4},{4,5},{5,6},{6,7},{7,8},{8,9},{9,10},{10,1... | collective-permute-start | bytes 49160 | tf_op jit(solution)/shard_map/ppermute | solution.py:33
  16.6 4.2 %collective-permute-start.2 = (bf16[64,128]{1,0:T(8,128)(2,1)S(1)}, bf16[64,128]{1,0:T(8,128)(2,1)S(1)}, u32[]{:S(2)}, u32[]{:S(2)}) collective-permute-start(bf16[64,128]{1,0:T(8,128)(2,1)S(1)} %collective-permute-done.1.fetched_ref), channel_id=1, source_target_pairs={{0,128},{1,129},{2,130},{3,131},{4,132},{5,133},{6,134},{7,135},{8... | collective-permute-start | bytes 49160 | tf_op jit(solution)/shard_map/ppermute | solution.py:33
  20.8 28.9 %copy-start = (bf16[1280,64]{0,1:T(8,128)(2,1)S(1)}, bf16[1280,64]{0,1:T(8,128)(2,1)}, u32[]{:S(2)}) copy-start(bf16[1280,64]{0,1:T(8,128)(2,1)} %param.9) | copy-start | bytes 491524
  20.8 29.1 %copy-start.1 = (f32[1280]{0:T(1024)S(1)}, f32[1280]{0:T(1024)}, u32[]{:S(2)}) copy-start(f32[1280]{0:T(1024)} %param.8) | copy-start | bytes 15364
  32.4 31.1 %all-to-all-start = ((bf16[128,3,2,128]{3,2,1,0:T(2,128)(2,1)}), bf16[128,3,2,128]{3,2,1,0:T(2,128)(2,1)S(1)}, u32[]{:S(2)}, u32[]{:S(2)}) async-start(bf16[128,3,2,128]{3,2,1,0:T(2,128)(2,1)} %bitcast.9), calls=%async_computation | async-start | bytes 393216 | tf_op jit(solution)/shard_map/all_to_all | solution.py:314

commit v4 on v3

--- a/solution.py
+++ b/solution.py
@@ -15,6 +15,7 @@
 NN = (((1,), (0,)), ((), ()))
 NT = (((1,), (1,)), ((), ()))
 TN = (((0,), (0,)), ((), ()))
+HINT = 8_000_000_000
 SENT_ROWS = 80
 GROUP = 4
 JOIN_FROM = 20
@@ -61,16 +62,15 @@
 
 
 def project_body(
-    hidden_hbm, gain_hbm, head_hbm, noise_hbm, frames_hbm, w_hbm, out_ref, noise_ref, hidden_ref,
-    frames_ref, w_ref, gain_ref, head_ref, sems,
+    hidden_hbm, gain_hbm, head_hbm, noise_hbm, frames_hbm, out_ref, noise_ref, hidden_ref,
+    frames_ref, gain_ref, head_ref, sems,
 ):
     features = hidden_ref.shape[1]
     pieces = [slice(i, i + 256) for i in range(0, features, 256)]
     copies = fetch(
         [(gain_hbm, gain_ref)]
         + [(hidden_hbm.at[:, piece], hidden_ref.at[:, piece]) for piece in pieces]
-        + [(head_hbm, head_ref), (noise_hbm, noise_ref), (frames_hbm, frames_ref)]
-        + [(w_hbm.at[0, i], w_ref.at[i]) for i in range(2)],
+        + [(head_hbm, head_ref), (noise_hbm, noise_ref), (frames_hbm, frames_ref)],
         sems,
     )
     copies[0].wait()
@@ -105,7 +105,7 @@
 
 def prepare_body(place_ref, w_ref, frames_ref, hidden_ref, fold_ref, bias_ref, spread_ref):
     scale = HS ** (-0.5) * math.log2(math.e)
-    heads = w_ref.shape[2] // HS
+    heads = w_ref.shape[3] // HS
     place = place_ref[0]
     blocks = frames_ref.shape[0]
     query_frame = frames_ref[pl.ds(place, 1), :]
@@ -135,17 +135,14 @@
     for h in range(heads):
         cols = slice(h * HS, (h + 1) * HS)
         fold_ref[h * 64 : (h + 1) * 64, :] = (
-            mm(w_ref[1, :, cols], w_ref[0, :, cols], NT) * scale
+            mm(w_ref[0, 1, :, cols], w_ref[0, 0, :, cols], NT) * scale
         ).astype(BF)
 
 
 def attend_body(
-    role_ref, before1_ref, fetched_ref, swapped_ref, own_ref, fold_ref, bias_ref, w_hbm, out_ref,
-    query_ref, mixed_ref, join_ref, w_ref, sems,
+    role_ref, before1_ref, fetched_ref, swapped_ref, own_ref, fold_ref, bias_ref, w_ref, out_ref,
+    query_ref, mixed_ref, join_ref,
 ):
-    values_copy, output_copy = fetch(
-        [(w_hbm.at[0, 2], w_ref.at[0]), (w_hbm.at[0, 3], w_ref.at[1])], sems
-    )
     heads = fold_ref.shape[0] // 64
     role = role_ref[0]
     own = own_ref[...]
@@ -178,13 +175,13 @@
         one, two = slice(h * HS, (h + 1) * HS), slice((h + 1) * HS, (h + 2) * HS)
         values = jnp.concatenate(
             [
-                jnp.concatenate([w_ref[0, :, one], zero], axis=1),
-                jnp.concatenate([zero, w_ref[0, :, two]], axis=1),
+                jnp.concatenate([w_ref[0, 2, :, one], zero], axis=1),
+                jnp.concatenate([zero, w_ref[0, 2, :, two]], axis=1),
             ],
             axis=0,
         )
         join_ref[:, h * 64 : (h + 2) * 64] = mm(
-            w_ref[1, :, h * HS : (h + 2) * HS], values, NT
+            w_ref[0, 3, :, h * HS : (h + 2) * HS], values, NT
         ).astype(BF)
 
     pairs = list(range(0, heads, 2))
@@ -194,9 +191,6 @@
         current = soften(scores) if h < heads else None
         if expo is not None:
             mix(h - GROUP, expo)
-        if h == JOIN_FROM:
-            values_copy.wait()
-            output_copy.wait()
         if h >= JOIN_FROM:
             for _ in range(-(-len(pairs) * GROUP // (heads + GROUP - h))):
                 join(pairs.pop(0))
@@ -239,7 +233,8 @@
 
 
 def finish_body(terms_ref, gain_ref, head_ref, head_grad_ref, gain_grad_ref):
-    total = jnp.sum(terms_ref[...].astype(F32), axis=0)
+    total = jnp.sum(terms_ref[...].astype(F32).reshape(-1, 24, 128), axis=0)
+    total = total[0:6] + total[6:12] + total[12:18] + total[18:24]
     rows = jnp.concatenate([total[0:5, 0:64], total[0:5, 64:128]], axis=0)
     head_grad_ref[...] = gain_ref[...] * rows
     column = jnp.sum(head_ref[...].astype(F32) * rows, axis=1, keepdims=True)
@@ -258,24 +253,20 @@
     role = lax.axis_index("role").astype(jnp.int32)
     phase = 0.5 * math.pi * timestep.astype(F32) / 1000.0
 
-    wide = score_weights.shape[2:]
-    sent, noise_t, hidden_v, frames_v, query_key = call(
+    sent, noise_t, hidden_v, frames_v = call(
         project_body,
         (
             shape((SENT_ROWS, tok_rows), BF), shape((64, tok_rows), BF), shape(hidden.shape, BF),
-            shape((blocks, tok_rows), jnp.int32), shape((2, *wide), BF),
+            shape((blocks, tok_rows), jnp.int32),
         ),
         *map(
             in_hbm,
-            (
-                hidden, gain_rows, head_t, noise.T, frames.reshape(blocks, tok_rows),
-                score_weights,
-            ),
+            (hidden, gain_rows, head_t, noise.T, frames.reshape(blocks, tok_rows)),
         ),
-        specs=[HBM] * 6,
+        specs=[HBM] * 5,
         scratch=[
             pltpu.VMEM(gain_rows.shape, F32), pltpu.VMEM(head_t.shape, BF),
-            pltpu.SemaphoreType.DMA((6 + features // 256,)),
+            pltpu.SemaphoreType.DMA((4 + features // 256,)),
         ],
     )
     parts = lax.all_gather(sent, "role")
@@ -283,6 +274,7 @@
         functools.partial(noisy_body, width),
         (shape((64, tok_rows), F32), shape((1, tok_rows), F32), shape((64, tok_rows), BF)),
         parts, noise_t, jnp.cos(phase), jnp.sin(phase), specs=[VMEM, VMEM, SMEM, SMEM], limit=2,
+        flops=HINT,
     )
     fetched = move(noisy, lambda r, s: (r, s + 2 if r % 2 == 0 else s - 1))
     before1 = move(noisy, lambda r, s: (r, s + 1))
@@ -290,16 +282,15 @@
     fold, bias, spread = call(
         prepare_body,
         (shape((2560, 64), BF), shape((512, 128), F32), shape((blocks * 6, 256), BF)),
-        place[None], query_key, frames_v, hidden_v, specs=[SMEM] + [VMEM] * 3,
-        flops=2_000_000_000,
+        place[None], score_weights, frames_v, hidden_v, specs=[SMEM] + [VMEM] * 3,
+        flops=1_000_000,
     )
     predicted = call(
         attend_body, shape((64, tok_rows), BF),
-        role[None], before1, fetched, swapped, noisy, fold, bias, in_hbm(score_weights),
-        specs=[SMEM] + [VMEM] * 6 + [HBM], flops=3_000_000_000, limit=24,
+        role[None], before1, fetched, swapped, noisy, fold, bias, score_weights,
+        specs=[SMEM] + [VMEM] * 7, flops=3_000_000_000, limit=24,
         scratch=[
             pltpu.VMEM((2560, 128), BF), pltpu.VMEM((2560, 128), BF), pltpu.VMEM((64, 2560), BF),
-            pltpu.VMEM((2, *wide), BF), pltpu.SemaphoreType.DMA((2,)),
         ],
     )
     gaps = lax.all_gather(predicted, "role")
@@ -311,7 +302,7 @@
         ),
         gaps, inverse, spread,
     )
-    summed = lax.all_to_all(terms.reshape(blocks, 3, 2, 128), "seq", 0, 0).reshape(blocks, 6, 128)
+    summed = lax.all_to_all(terms.reshape(blocks, 3, 2, 128), "seq", 0, 0).reshape(blocks * 6, 128)
     hidden_grad, latent = call(
         functools.partial(hidden_grad_body, width), (shape(hidden.shape, BF), shape((64, tok_rows), BF)),
         gap, projected, inverse, scaled, head_t, gain_rows, hidden_v, flops=1_000_000_000,

time: 64.9 us -> 64.1 us (0.988)
  Pallas kernels: 9.19 us -> 8.45 us
    pallas_call x7, Pallas kernels: 9.19 us -> 8.45 us  [call(): pl.pallas_call(body, out_shape=outs, in_specs=specs or [VMEM] * len(args)...]
where the time goes in v4:
time: 64.1 us; the launch traced here: 63.8 us
  starting transfers between devices  25 us (39%)
  blocking collectives  16.1 us (25%)
  waiting for transfers between devices  12.4 us (19%)
  Pallas kernels  8.45 us (13%)
  between operations  1.56 us (2%)
    all_to_all x1, starting transfers between devices, local(): lax.all_to_all(terms.reshape(blocks, 3, 2, 128), 'seq', 0, 0)  17.3 us
    all_to_all x1, waiting for transfers between devices, local(): lax.all_to_all(terms.reshape(blocks, 3, 2, 128), 'seq', 0, 0)  12.4 us
    all_gather x1, blocking collectives, local(): parts = lax.all_gather(sent, 'role')  9.16 us
    pallas_call x7, Pallas kernels, call(): pl.pallas_call(body, out_shape=outs, in_specs=specs or [VMEM] * len(args)...  8.45 us
    ppermute x3, starting transfers between devices, move(): return lax.ppermute(block, ('role', 'seq'), route)  7.66 us
    all_gather x1, blocking collectives, local(): gaps = lax.all_gather(predicted, 'role')  6.94 us
  transfers between devices with their start and end apart: 4, of which 1 were waited for; matrix products, arithmetic and copies ran while one was open for 1% of the time, Pallas kernels for 3%

profile of v4, /device:TPU:4, one launch (start us, length us, event | category | flops | bytes accessed | tf_op | source)
XLA Modules:
  0.0 63.8 jit_solution(7760452700780263852)
XLA Ops:
  1.4 1.4 %shard_map.102 = (bf16[80,128]{1,0:T(8,128)(2,1)S(1)}, bf16[64,128]{1,0:T(8,128)(2,1)S(1)}, bf16[128,1280]{1,0:T(8,128)(2,1)S(1)}, s32[128,128]{1,0:T(8,128)S(1)}) custom-call(bf16[128,1280]{1,0:T(8,128)(2,1)} %hidden_hbm.1, f32[10,128]{1,0:T(8,128)} %bitcast.19, bf16[64,1280]{1,0:T(8,128)(2,1)} %bitcast.16, bf16[64,128]{1,0:T(8,128)(2,1)} %bitcast.22, ...), custom_call_target="tpu_custom_call" | custom-call | bytes 578560 | tf_op jit(solution)/shard_map/pallas_call | solution.py:43
  2.9 9.2 %all-gather = bf16[320,128]{1,0:T(8,128)(2,1)S(1)} all-gather(bf16[80,128]{1,0:T(8,128)(2,1)S(1)} %get-tuple-element.21), channel_id=2, replica_groups=mesh['role'=4,'seq'=128] {'role'}, dimensions={0}, use_global_device_ids=true | all-gather | bytes 102400 | tf_op jit(solution)/shard_map/all_gather | solution.py:272
  12.0 0.0 copy-start
  12.1 1.4 %collective-permute-start.1 = (bf16[64,128]{1,0:T(8,128)(2,1)S(1)}, bf16[64,128]{1,0:T(8,128)(2,1)S(1)}, u32[]{:S(2)}, u32[]{:S(2)}) collective-permute-start(bf16[64,128]{1,0:T(8,128)(2,1)S(1)} %get-tuple-element.23.own_ref), channel_id=1, source_target_pairs={{0,2},{1,3},{2,4},{3,5},{4,6},{5,7},{6,8},{7,9},{8,10},{9,11},{10,... | collective-permute-start | bytes 49160 | tf_op jit(solution)/shard_map/ppermute | solution.py:34
  13.5 2.9 %collective-permute-start = (bf16[64,128]{1,0:T(8,128)(2,1)S(1)}, bf16[64,128]{1,0:T(8,128)(2,1)S(1)}, u32[]{:S(2)}, u32[]{:S(2)}) collective-permute-start(bf16[64,128]{1,0:T(8,128)(2,1)S(1)} %get-tuple-element.23.own_ref), channel_id=1, source_target_pairs={{0,1},{1,2},{2,3},{3,4},{4,5},{5,6},{6,7},{7,8},{8,9},{9,10},{10,1... | collective-permute-start | bytes 49160 | tf_op jit(solution)/shard_map/ppermute | solution.py:34
  16.4 0.0 collective-permute-done.1.fetched_ref
  16.4 3.3 %collective-permute-start.2 = (bf16[64,128]{1,0:T(8,128)(2,1)S(1)}, bf16[64,128]{1,0:T(8,128)(2,1)S(1)}, u32[]{:S(2)}, u32[]{:S(2)}) collective-permute-start(bf16[64,128]{1,0:T(8,128)(2,1)S(1)} %collective-permute-done.1.fetched_ref), channel_id=1, source_target_pairs={{0,128},{1,129},{2,130},{3,131},{4,132},{5,133},{6,134},{7,135},{8... | collective-permute-start | bytes 49160 | tf_op jit(solution)/shard_map/ppermute | solution.py:34
  19.8 0.0 copy-done
  19.8 0.9 %shard_map.104 = (bf16[2560,64]{1,0:T(8,128)(2,1)S(1)}, f32[512,128]{1,0:T(8,128)S(1)}, bf16[768,256]{1,0:T(8,128)(2,1)S(1)}) custom-call(s32[1]{0:T(128)} %bitcast.6.place_ref, bf16[1,4,64,5120]{3,2,1,0:T(8,128)(2,1)S(1)} %copy-done, s32[128,128]{1,0:T(8,128)S(1)} %get-tuple-element.24.frames_ref, bf16[128,1280]{1,0:T(8,128)(2,1)S(1)} %get-tuple-element.25.hidden_ref), custom_call_target="tpu_custom_call" | custom-call | flops 1000000 | bytes 3014660 | tf_op jit(solution)/shard_map/pallas_call | solution.py:43
  20.6 0.0 collective-permute-done.before1_ref
  20.6 0.0 collective-permute-done.2.swapped_ref
  20.7 0.0 copy-start.1
  20.7 0.0 copy-start.2
  20.7 3.3 %shard_map.105 = bf16[64,128]{1,0:T(8,128)(2,1)S(1)} custom-call(s32[1]{0:T(128)} %bitcast.role_ref, bf16[64,128]{1,0:T(8,128)(2,1)S(1)} %collective-permute-done.before1_ref, bf16[64,128]{1,0:T(8,128)(2,1)S(1)} %collective-permute-done.1.fetched_ref, bf16[64,128]{1,0:T(8,128)(2,1)S(1)} %collective-permute-done.2.swapped_ref, ...), custom_call_target="tpu_custom_call" | custom-call | flops 3000000000 | bytes 3276804 | tf_op jit(solution)/shard_map/pallas_call | solution.py:43
  24.0 6.9 %all-gather.1 = bf16[256,128]{1,0:T(8,128)(2,1)S(1)} all-gather(bf16[64,128]{1,0:T(8,128)(2,1)S(1)} %shard_map.105), channel_id=3, replica_groups=mesh['role'=4,'seq'=128] {'role'}, dimensions={0}, use_global_device_ids=true | all-gather | bytes 81920 | tf_op jit(solution)/shard_map/all_gather | solution.py:296
  30.9 1.0 %shard_map.106 = (f32[64,128]{1,0:T(8,128)S(1)}, bf16[64,128]{1,0:T(8,128)(2,1)S(1)}, bf16[768,128]{1,0:T(8,128)(2,1)}) custom-call(bf16[4,64,128]{2,1,0:T(8,128)(2,1)S(1)} %bitcast.15, f32[1,128]{1,0:T(1,128)S(1)} %get-tuple-element.28.inv_ref, bf16[768,256]{1,0:T(8,128)(2,1)S(1)} %get-tuple-element.29.spread_ref), custom_call_target="tpu_custom_call" | custom-call | bytes 459264 | tf_op jit(solution)/shard_map/pallas_call | solution.py:43
  31.9 17.3 %all-to-all-start = ((bf16[128,3,2,128]{3,2,1,0:T(2,128)(2,1)}), bf16[128,3,2,128]{3,2,1,0:T(2,128)(2,1)S(1)}, u32[]{:S(2)}, u32[]{:S(2)}) async-start(bf16[128,3,2,128]{3,2,1,0:T(2,128)(2,1)} %bitcast.9), calls=%async_computation | async-start | bytes 393216 | tf_op jit(solution)/shard_map/all_to_all | solution.py:305
  49.2 0.0 copy-done.1
  49.2 0.1 constant_dynamic-slice_fusion
  49.3 0.1 copy.13.head_ref
  49.4 0.0 copy-done.2
  49.4 0.1 dynamic-slice_bitcast_fusion
  49.5 0.1 copy.12.gain_ref
  49.6 1.0 %shard_map.107 = (bf16[128,1280]{1,0:T(8,128)(2,1)}, bf16[64,128]{1,0:T(8,128)(2,1)}) custom-call(f32[64,128]{1,0:T(8,128)S(1)} %get-tuple-element.30.gap_ref, f32[64,128]{1,0:T(8,128)S(1)} %get-tuple-element.31.proj_ref, f32[1,128]{1,0:T(1,128)S(1)} %get-tuple-element.28.inv_ref, bf16[64,128]{1,0:T(8,128)(2,1)S(1)} %get-tuple-element.32.scaled_ref, ...), custom_call_target="tpu_custom_call" | custom-call | flops 1000000000 | bytes 579072 | tf_op jit(solution)/shard_map/pallas_call | solution.py:43
  50.6 12.4 %all-to-all-done = bf16[128,3,2,128]{3,2,1,0:T(2,128)(2,1)S(1)} async-done(((bf16[128,3,2,128]{3,2,1,0:T(2,128)(2,1)}), bf16[128,3,2,128]{3,2,1,0:T(2,128)(2,1)S(1)}, u32[]{:S(2)}, u32[]{:S(2)}) %all-to-all-start) | async-done | bytes 196640 | tf_op jit(solution)/shard_map/all_to_all | solution.py:305
  63.0 0.9 %shard_map.108 = (f32[10,64]{1,0:T(8,128)}, f32[1,10]{1,0:T(1,128)}) custom-call(bf16[768,128]{1,0:T(8,128)(2,1)S(1)} %bitcast.14, f32[10,1]{1,0:T(8,128)S(1)} %copy.12.gain_ref, bf16[10,64]{1,0:T(8,128)(2,1)S(1)} %copy.13.head_ref), custom_call_target="tpu_custom_call" | custom-call | bytes 197928 | tf_op jit(solution)/shard_map/pallas_call | solution.py:43
  (1 shorter events, 0.0 us)
Async XLA Ops:
  12.0 7.7 %copy-start = (bf16[1,4,64,5120]{3,2,1,0:T(8,128)(2,1)S(1)}, bf16[1,4,64,5120]{3,2,1,0:T(8,128)(2,1)}, u32[]{:S(2)}) copy-start(bf16[1,4,64,5120]{3,2,1,0:T(8,128)(2,1)} %w_ref.3) | copy-start | bytes 7864324
  12.1 4.4 %collective-permute-start.1 = (bf16[64,128]{1,0:T(8,128)(2,1)S(1)}, bf16[64,128]{1,0:T(8,128)(2,1)S(1)}, u32[]{:S(2)}, u32[]{:S(2)}) collective-permute-start(bf16[64,128]{1,0:T(8,128)(2,1)S(1)} %get-tuple-element.23.own_ref), channel_id=1, source_target_pairs={{0,2},{1,3},{2,4},{3,5},{4,6},{5,7},{6,8},{7,9},{8,10},{9,11},{10,... | collective-permute-start | bytes 49160 | tf_op jit(solution)/shard_map/ppermute | solution.py:34
  13.5 7.2 %collective-permute-start = (bf16[64,128]{1,0:T(8,128)(2,1)S(1)}, bf16[64,128]{1,0:T(8,128)(2,1)S(1)}, u32[]{:S(2)}, u32[]{:S(2)}) collective-permute-start(bf16[64,128]{1,0:T(8,128)(2,1)S(1)} %get-tuple-element.23.own_ref), channel_id=1, source_target_pairs={{0,1},{1,2},{2,3},{3,4},{4,5},{5,6},{6,7},{7,8},{8,9},{9,10},{10,1... | collective-permute-start | bytes 49160 | tf_op jit(solution)/shard_map/ppermute | solution.py:34
  16.4 4.2 %collective-permute-start.2 = (bf16[64,128]{1,0:T(8,128)(2,1)S(1)}, bf16[64,128]{1,0:T(8,128)(2,1)S(1)}, u32[]{:S(2)}, u32[]{:S(2)}) collective-permute-start(bf16[64,128]{1,0:T(8,128)(2,1)S(1)} %collective-permute-done.1.fetched_ref), channel_id=1, source_target_pairs={{0,128},{1,129},{2,130},{3,131},{4,132},{5,133},{6,134},{7,135},{8... | collective-permute-start | bytes 49160 | tf_op jit(solution)/shard_map/ppermute | solution.py:34
  20.7 28.5 %copy-start.1 = (bf16[1280,64]{0,1:T(8,128)(2,1)S(1)}, bf16[1280,64]{0,1:T(8,128)(2,1)}, u32[]{:S(2)}) copy-start(bf16[1280,64]{0,1:T(8,128)(2,1)} %param.9) | copy-start | bytes 491524
  20.7 28.7 %copy-start.2 = (f32[1280]{0:T(1024)S(1)}, f32[1280]{0:T(1024)}, u32[]{:S(2)}) copy-start(f32[1280]{0:T(1024)} %param.8) | copy-start | bytes 15364
  31.9 31.1 %all-to-all-start = ((bf16[128,3,2,128]{3,2,1,0:T(2,128)(2,1)}), bf16[128,3,2,128]{3,2,1,0:T(2,128)(2,1)S(1)}, u32[]{:S(2)}, u32[]{:S(2)}) async-start(bf16[128,3,2,128]{3,2,1,0:T(2,128)(2,1)} %bitcast.9), calls=%async_computation | async-start | bytes 393216 | tf_op jit(solution)/shard_map/all_to_all | solution.py:305

commit v5 on v4

--- a/solution.py
+++ b/solution.py
@@ -18,7 +18,6 @@
 HINT = 8_000_000_000
 SENT_ROWS = 80
 GROUP = 4
-JOIN_FROM = 20
 VMEM, SMEM = pl.BlockSpec(memory_space=pltpu.VMEM), pl.BlockSpec(memory_space=pltpu.SMEM)
 HBM = pl.BlockSpec(memory_space=pltpu.HBM)
 
@@ -191,9 +190,8 @@
         current = soften(scores) if h < heads else None
         if expo is not None:
             mix(h - GROUP, expo)
-        if h >= JOIN_FROM:
-            for _ in range(-(-len(pairs) * GROUP // (heads + GROUP - h))):
-                join(pairs.pop(0))
+        for _ in range(-(-len(pairs) * GROUP // (heads + GROUP - h))):
+            join(pairs.pop(0))
         scores, expo = upcoming, current
     predicted = own.astype(F32) + mm(join_ref[...], mixed_ref[...])
     weight = jnp.float32(DIFF_TABLE[0])

time: 64.1 us -> 64 us (level)
  no operation moved by 1% of the time
where the time goes in v5:
time: 64 us; the launch traced here: 63.7 us
  starting transfers between devices  25 us (39%)
  blocking collectives  16.1 us (25%)
  waiting for transfers between devices  12.4 us (19%)
  Pallas kernels  8.28 us (13%)
  between operations  1.55 us (2%)
    all_to_all x1, starting transfers between devices, local(): lax.all_to_all(terms.reshape(blocks, 3, 2, 128), 'seq', 0, 0)  17.3 us
    all_to_all x1, waiting for transfers between devices, local(): lax.all_to_all(terms.reshape(blocks, 3, 2, 128), 'seq', 0, 0)  12.4 us
    all_gather x1, blocking collectives, local(): parts = lax.all_gather(sent, 'role')  9.16 us
    pallas_call x7, Pallas kernels, call(): pl.pallas_call(body, out_shape=outs, in_specs=specs or [VMEM] * len(args)...  8.28 us
    ppermute x3, starting transfers between devices, move(): return lax.ppermute(block, ('role', 'seq'), route)  7.66 us
    all_gather x1, blocking collectives, local(): gaps = lax.all_gather(predicted, 'role')  6.94 us
  transfers between devices with their start and end apart: 4, of which 1 were waited for; matrix products, arithmetic and copies ran while one was open for 1% of the time, Pallas kernels for 3%

profile of v5, /device:TPU:4, one launch (start us, length us, event | category | flops | bytes accessed | tf_op | source)
XLA Modules:
  0.0 63.7 jit_solution(11119718363391737672)
XLA Ops:
  1.4 1.4 %shard_map.102 = (bf16[80,128]{1,0:T(8,128)(2,1)S(1)}, bf16[64,128]{1,0:T(8,128)(2,1)S(1)}, bf16[128,1280]{1,0:T(8,128)(2,1)S(1)}, s32[128,128]{1,0:T(8,128)S(1)}) custom-call(bf16[128,1280]{1,0:T(8,128)(2,1)} %hidden_hbm.1, f32[10,128]{1,0:T(8,128)} %bitcast.19, bf16[64,1280]{1,0:T(8,128)(2,1)} %bitcast.16, bf16[64,128]{1,0:T(8,128)(2,1)} %bitcast.22, ...), custom_call_target="tpu_custom_call" | custom-call | bytes 578560 | tf_op jit(solution)/shard_map/pallas_call | solution.py:42
  2.9 9.2 %all-gather = bf16[320,128]{1,0:T(8,128)(2,1)S(1)} all-gather(bf16[80,128]{1,0:T(8,128)(2,1)S(1)} %get-tuple-element.21), channel_id=2, replica_groups=mesh['role'=4,'seq'=128] {'role'}, dimensions={0}, use_global_device_ids=true | all-gather | bytes 102400 | tf_op jit(solution)/shard_map/all_gather | solution.py:270
  12.0 0.0 copy-start
  12.1 1.4 %collective-permute-start.1 = (bf16[64,128]{1,0:T(8,128)(2,1)S(1)}, bf16[64,128]{1,0:T(8,128)(2,1)S(1)}, u32[]{:S(2)}, u32[]{:S(2)}) collective-permute-start(bf16[64,128]{1,0:T(8,128)(2,1)S(1)} %get-tuple-element.23.own_ref), channel_id=1, source_target_pairs={{0,2},{1,3},{2,4},{3,5},{4,6},{5,7},{6,8},{7,9},{8,10},{9,11},{10,... | collective-permute-start | bytes 49160 | tf_op jit(solution)/shard_map/ppermute | solution.py:33
  13.5 2.9 %collective-permute-start = (bf16[64,128]{1,0:T(8,128)(2,1)S(1)}, bf16[64,128]{1,0:T(8,128)(2,1)S(1)}, u32[]{:S(2)}, u32[]{:S(2)}) collective-permute-start(bf16[64,128]{1,0:T(8,128)(2,1)S(1)} %get-tuple-element.23.own_ref), channel_id=1, source_target_pairs={{0,1},{1,2},{2,3},{3,4},{4,5},{5,6},{6,7},{7,8},{8,9},{9,10},{10,1... | collective-permute-start | bytes 49160 | tf_op jit(solution)/shard_map/ppermute | solution.py:33
  16.4 0.0 collective-permute-done.1.fetched_ref
  16.4 3.3 %collective-permute-start.2 = (bf16[64,128]{1,0:T(8,128)(2,1)S(1)}, bf16[64,128]{1,0:T(8,128)(2,1)S(1)}, u32[]{:S(2)}, u32[]{:S(2)}) collective-permute-start(bf16[64,128]{1,0:T(8,128)(2,1)S(1)} %collective-permute-done.1.fetched_ref), channel_id=1, source_target_pairs={{0,128},{1,129},{2,130},{3,131},{4,132},{5,133},{6,134},{7,135},{8... | collective-permute-start | bytes 49160 | tf_op jit(solution)/shard_map/ppermute | solution.py:33
  19.8 0.0 copy-done
  19.8 0.9 %shard_map.104 = (bf16[2560,64]{1,0:T(8,128)(2,1)S(1)}, f32[512,128]{1,0:T(8,128)S(1)}, bf16[768,256]{1,0:T(8,128)(2,1)S(1)}) custom-call(s32[1]{0:T(128)} %bitcast.6.place_ref, bf16[1,4,64,5120]{3,2,1,0:T(8,128)(2,1)S(1)} %copy-done, s32[128,128]{1,0:T(8,128)S(1)} %get-tuple-element.24.frames_ref, bf16[128,1280]{1,0:T(8,128)(2,1)S(1)} %get-tuple-element.25.hidden_ref), custom_call_target="tpu_custom_call" | custom-call | flops 1000000 | bytes 3014660 | tf_op jit(solution)/shard_map/pallas_call | solution.py:42
  20.6 0.0 collective-permute-done.before1_ref
  20.6 0.0 collective-permute-done.2.swapped_ref
  20.7 0.0 copy-start.1
  20.7 0.0 copy-start.2
  20.7 3.1 %shard_map.105 = bf16[64,128]{1,0:T(8,128)(2,1)S(1)} custom-call(s32[1]{0:T(128)} %bitcast.role_ref, bf16[64,128]{1,0:T(8,128)(2,1)S(1)} %collective-permute-done.before1_ref, bf16[64,128]{1,0:T(8,128)(2,1)S(1)} %collective-permute-done.1.fetched_ref, bf16[64,128]{1,0:T(8,128)(2,1)S(1)} %collective-permute-done.2.swapped_ref, ...), custom_call_target="tpu_custom_call" | custom-call | flops 3000000000 | bytes 3276804 | tf_op jit(solution)/shard_map/pallas_call | solution.py:42
  23.8 6.9 %all-gather.1 = bf16[256,128]{1,0:T(8,128)(2,1)S(1)} all-gather(bf16[64,128]{1,0:T(8,128)(2,1)S(1)} %shard_map.105), channel_id=3, replica_groups=mesh['role'=4,'seq'=128] {'role'}, dimensions={0}, use_global_device_ids=true | all-gather | bytes 81920 | tf_op jit(solution)/shard_map/all_gather | solution.py:294
  30.8 0.9 %shard_map.106 = (f32[64,128]{1,0:T(8,128)S(1)}, bf16[64,128]{1,0:T(8,128)(2,1)S(1)}, bf16[768,128]{1,0:T(8,128)(2,1)}) custom-call(bf16[4,64,128]{2,1,0:T(8,128)(2,1)S(1)} %bitcast.15, f32[1,128]{1,0:T(1,128)S(1)} %get-tuple-element.28.inv_ref, bf16[768,256]{1,0:T(8,128)(2,1)S(1)} %get-tuple-element.29.spread_ref), custom_call_target="tpu_custom_call" | custom-call | bytes 459264 | tf_op jit(solution)/shard_map/pallas_call | solution.py:42
  31.7 17.3 %all-to-all-start = ((bf16[128,3,2,128]{3,2,1,0:T(2,128)(2,1)}), bf16[128,3,2,128]{3,2,1,0:T(2,128)(2,1)S(1)}, u32[]{:S(2)}, u32[]{:S(2)}) async-start(bf16[128,3,2,128]{3,2,1,0:T(2,128)(2,1)} %bitcast.9), calls=%async_computation | async-start | bytes 393216 | tf_op jit(solution)/shard_map/all_to_all | solution.py:303
  49.0 0.0 copy-done.1
  49.0 0.1 constant_dynamic-slice_fusion
  49.1 0.1 copy.13.head_ref
  49.2 0.0 copy-done.2
  49.2 0.1 dynamic-slice_bitcast_fusion
  49.3 0.1 copy.12.gain_ref
  49.4 1.0 %shard_map.107 = (bf16[128,1280]{1,0:T(8,128)(2,1)}, bf16[64,128]{1,0:T(8,128)(2,1)}) custom-call(f32[64,128]{1,0:T(8,128)S(1)} %get-tuple-element.30.gap_ref, f32[64,128]{1,0:T(8,128)S(1)} %get-tuple-element.31.proj_ref, f32[1,128]{1,0:T(1,128)S(1)} %get-tuple-element.28.inv_ref, bf16[64,128]{1,0:T(8,128)(2,1)S(1)} %get-tuple-element.32.scaled_ref, ...), custom_call_target="tpu_custom_call" | custom-call | flops 1000000000 | bytes 579072 | tf_op jit(solution)/shard_map/pallas_call | solution.py:42
  50.4 12.4 %all-to-all-done = bf16[128,3,2,128]{3,2,1,0:T(2,128)(2,1)S(1)} async-done(((bf16[128,3,2,128]{3,2,1,0:T(2,128)(2,1)}), bf16[128,3,2,128]{3,2,1,0:T(2,128)(2,1)S(1)}, u32[]{:S(2)}, u32[]{:S(2)}) %all-to-all-start) | async-done | bytes 196640 | tf_op jit(solution)/shard_map/all_to_all | solution.py:303
  62.8 0.9 %shard_map.108 = (f32[10,64]{1,0:T(8,128)}, f32[1,10]{1,0:T(1,128)}) custom-call(bf16[768,128]{1,0:T(8,128)(2,1)S(1)} %bitcast.14, f32[10,1]{1,0:T(8,128)S(1)} %copy.12.gain_ref, bf16[10,64]{1,0:T(8,128)(2,1)S(1)} %copy.13.head_ref), custom_call_target="tpu_custom_call" | custom-call | bytes 197928 | tf_op jit(solution)/shard_map/pallas_call | solution.py:42
  (1 shorter events, 0.0 us)
Async XLA Ops:
  12.0 7.7 %copy-start = (bf16[1,4,64,5120]{3,2,1,0:T(8,128)(2,1)S(1)}, bf16[1,4,64,5120]{3,2,1,0:T(8,128)(2,1)}, u32[]{:S(2)}) copy-start(bf16[1,4,64,5120]{3,2,1,0:T(8,128)(2,1)} %w_ref.3) | copy-start | bytes 7864324
  12.1 4.4 %collective-permute-start.1 = (bf16[64,128]{1,0:T(8,128)(2,1)S(1)}, bf16[64,128]{1,0:T(8,128)(2,1)S(1)}, u32[]{:S(2)}, u32[]{:S(2)}) collective-permute-start(bf16[64,128]{1,0:T(8,128)(2,1)S(1)} %get-tuple-element.23.own_ref), channel_id=1, source_target_pairs={{0,2},{1,3},{2,4},{3,5},{4,6},{5,7},{6,8},{7,9},{8,10},{9,11},{10,... | collective-permute-start | bytes 49160 | tf_op jit(solution)/shard_map/ppermute | solution.py:33
  13.5 7.2 %collective-permute-start = (bf16[64,128]{1,0:T(8,128)(2,1)S(1)}, bf16[64,128]{1,0:T(8,128)(2,1)S(1)}, u32[]{:S(2)}, u32[]{:S(2)}) collective-permute-start(bf16[64,128]{1,0:T(8,128)(2,1)S(1)} %get-tuple-element.23.own_ref), channel_id=1, source_target_pairs={{0,1},{1,2},{2,3},{3,4},{4,5},{5,6},{6,7},{7,8},{8,9},{9,10},{10,1... | collective-permute-start | bytes 49160 | tf_op jit(solution)/shard_map/ppermute | solution.py:33
  16.4 4.2 %collective-permute-start.2 = (bf16[64,128]{1,0:T(8,128)(2,1)S(1)}, bf16[64,128]{1,0:T(8,128)(2,1)S(1)}, u32[]{:S(2)}, u32[]{:S(2)}) collective-permute-start(bf16[64,128]{1,0:T(8,128)(2,1)S(1)} %collective-permute-done.1.fetched_ref), channel_id=1, source_target_pairs={{0,128},{1,129},{2,130},{3,131},{4,132},{5,133},{6,134},{7,135},{8... | collective-permute-start | bytes 49160 | tf_op jit(solution)/shard_map/ppermute | solution.py:33
  20.7 28.4 %copy-start.1 = (bf16[1280,64]{0,1:T(8,128)(2,1)S(1)}, bf16[1280,64]{0,1:T(8,128)(2,1)}, u32[]{:S(2)}) copy-start(bf16[1280,64]{0,1:T(8,128)(2,1)} %param.9) | copy-start | bytes 491524
  20.7 28.5 %copy-start.2 = (f32[1280]{0:T(1024)S(1)}, f32[1280]{0:T(1024)}, u32[]{:S(2)}) copy-start(f32[1280]{0:T(1024)} %param.8) | copy-start | bytes 15364
  31.7 31.1 %all-to-all-start = ((bf16[128,3,2,128]{3,2,1,0:T(2,128)(2,1)}), bf16[128,3,2,128]{3,2,1,0:T(2,128)(2,1)S(1)}, u32[]{:S(2)}, u32[]{:S(2)}) async-start(bf16[128,3,2,128]{3,2,1,0:T(2,128)(2,1)} %bitcast.9), calls=%async_computation | async-start | bytes 393216 | tf_op jit(solution)/shard_map/all_to_all | solution.py:303

commit v6 on v5

--- a/solution.py
+++ b/solution.py
@@ -67,21 +67,23 @@
     features = hidden_ref.shape[1]
     pieces = [slice(i, i + 256) for i in range(0, features, 256)]
     copies = fetch(
-        [(gain_hbm, gain_ref)]
+        [(gain_hbm, gain_ref), (head_hbm, head_ref)]
         + [(hidden_hbm.at[:, piece], hidden_ref.at[:, piece]) for piece in pieces]
-        + [(head_hbm, head_ref), (noise_hbm, noise_ref), (frames_hbm, frames_ref)],
+        + [(noise_hbm, noise_ref), (frames_hbm, frames_ref)],
         sems,
     )
     copies[0].wait()
-    gained, lanes = [], 0.0
-    for i in range(features // 128):
-        if i % 2 == 0:
-            copies[1 + i // 2].wait()
-        hidden = hidden_ref[:, i * 128 : (i + 1) * 128].astype(F32)
-        gained.append((hidden * gain_ref[i : i + 1, :]).astype(BF))
-        lanes = lanes + hidden * hidden
-    copies[1 + len(pieces)].wait()
-    out_ref[0:64, :] = mm(head_ref[...], jnp.concatenate(gained, axis=1), NT).astype(BF)
+    copies[1].wait()
+    projected, lanes = 0.0, 0.0
+    for copy, piece in zip(copies[2:], pieces):
+        copy.wait()
+        gained = []
+        for i in range(piece.start // 128, piece.stop // 128):
+            hidden = hidden_ref[:, i * 128 : (i + 1) * 128].astype(F32)
+            gained.append((hidden * gain_ref[i : i + 1, :]).astype(BF))
+            lanes = lanes + hidden * hidden
+        projected = projected + mm(head_ref[:, piece], jnp.concatenate(gained, axis=1), NT)
+    out_ref[0:64, :] = projected.astype(BF)
     total = jnp.sum(lanes.T, axis=0, keepdims=True)
     high = total.astype(BF).astype(F32)
     row = lax.broadcasted_iota(jnp.int32, (16, 128), 0)

time: 64 us -> 64.2 us (level)
  no operation moved by 1% of the time
where the time goes in v6:
time: 64.2 us; the launch traced here: 63.9 us
  starting transfers between devices  25 us (39%)
  blocking collectives  16.1 us (25%)
  waiting for transfers between devices  12.4 us (19%)
  Pallas kernels  8.48 us (13%)
  between operations  1.55 us (2%)
    all_to_all x1, starting transfers between devices, local(): lax.all_to_all(terms.reshape(blocks, 3, 2, 128), 'seq', 0, 0)  17.3 us
    all_to_all x1, waiting for transfers between devices, local(): lax.all_to_all(terms.reshape(blocks, 3, 2, 128), 'seq', 0, 0)  12.4 us
    all_gather x1, blocking collectives, local(): parts = lax.all_gather(sent, 'role')  9.16 us
    pallas_call x7, Pallas kernels, call(): pl.pallas_call(body, out_shape=outs, in_specs=specs or [VMEM] * len(args)...  8.48 us
    ppermute x3, starting transfers between devices, move(): return lax.ppermute(block, ('role', 'seq'), route)  7.66 us
    all_gather x1, blocking collectives, local(): gaps = lax.all_gather(predicted, 'role')  6.94 us
  transfers between devices with their start and end apart: 4, of which 1 were waited for; matrix products, arithmetic and copies ran while one was open for 1% of the time, Pallas kernels for 3%

profile of v6, /device:TPU:4, one launch (start us, length us, event | category | flops | bytes accessed | tf_op | source)
XLA Modules:
  0.0 63.9 jit_solution(2205507931899100034)
XLA Ops:
  1.4 1.6 %shard_map.102 = (bf16[80,128]{1,0:T(8,128)(2,1)S(1)}, bf16[64,128]{1,0:T(8,128)(2,1)S(1)}, bf16[128,1280]{1,0:T(8,128)(2,1)S(1)}, s32[128,128]{1,0:T(8,128)S(1)}) custom-call(bf16[128,1280]{1,0:T(8,128)(2,1)} %hidden_hbm.1, f32[10,128]{1,0:T(8,128)} %bitcast.19, bf16[64,1280]{1,0:T(8,128)(2,1)} %bitcast.16, bf16[64,128]{1,0:T(8,128)(2,1)} %bitcast.22, ...), custom_call_target="tpu_custom_call" | custom-call | bytes 578560 | tf_op jit(solution)/shard_map/pallas_call | solution.py:42
  3.1 9.2 %all-gather = bf16[320,128]{1,0:T(8,128)(2,1)S(1)} all-gather(bf16[80,128]{1,0:T(8,128)(2,1)S(1)} %get-tuple-element.21), channel_id=2, replica_groups=mesh['role'=4,'seq'=128] {'role'}, dimensions={0}, use_global_device_ids=true | all-gather | bytes 102400 | tf_op jit(solution)/shard_map/all_gather | solution.py:272
  12.2 0.0 copy-start
  12.3 1.4 %collective-permute-start.1 = (bf16[64,128]{1,0:T(8,128)(2,1)S(1)}, bf16[64,128]{1,0:T(8,128)(2,1)S(1)}, u32[]{:S(2)}, u32[]{:S(2)}) collective-permute-start(bf16[64,128]{1,0:T(8,128)(2,1)S(1)} %get-tuple-element.23.own_ref), channel_id=1, source_target_pairs={{0,2},{1,3},{2,4},{3,5},{4,6},{5,7},{6,8},{7,9},{8,10},{9,11},{10,... | collective-permute-start | bytes 49160 | tf_op jit(solution)/shard_map/ppermute | solution.py:33
  13.7 2.9 %collective-permute-start = (bf16[64,128]{1,0:T(8,128)(2,1)S(1)}, bf16[64,128]{1,0:T(8,128)(2,1)S(1)}, u32[]{:S(2)}, u32[]{:S(2)}) collective-permute-start(bf16[64,128]{1,0:T(8,128)(2,1)S(1)} %get-tuple-element.23.own_ref), channel_id=1, source_target_pairs={{0,1},{1,2},{2,3},{3,4},{4,5},{5,6},{6,7},{7,8},{8,9},{9,10},{10,1... | collective-permute-start | bytes 49160 | tf_op jit(solution)/shard_map/ppermute | solution.py:33
  16.6 0.0 collective-permute-done.1.fetched_ref
  16.6 3.3 %collective-permute-start.2 = (bf16[64,128]{1,0:T(8,128)(2,1)S(1)}, bf16[64,128]{1,0:T(8,128)(2,1)S(1)}, u32[]{:S(2)}, u32[]{:S(2)}) collective-permute-start(bf16[64,128]{1,0:T(8,128)(2,1)S(1)} %collective-permute-done.1.fetched_ref), channel_id=1, source_target_pairs={{0,128},{1,129},{2,130},{3,131},{4,132},{5,133},{6,134},{7,135},{8... | collective-permute-start | bytes 49160 | tf_op jit(solution)/shard_map/ppermute | solution.py:33
  20.0 0.0 copy-done
  20.0 0.9 %shard_map.104 = (bf16[2560,64]{1,0:T(8,128)(2,1)S(1)}, f32[512,128]{1,0:T(8,128)S(1)}, bf16[768,256]{1,0:T(8,128)(2,1)S(1)}) custom-call(s32[1]{0:T(128)} %bitcast.6.place_ref, bf16[1,4,64,5120]{3,2,1,0:T(8,128)(2,1)S(1)} %copy-done, s32[128,128]{1,0:T(8,128)S(1)} %get-tuple-element.24.frames_ref, bf16[128,1280]{1,0:T(8,128)(2,1)S(1)} %get-tuple-element.25.hidden_ref), custom_call_target="tpu_custom_call" | custom-call | flops 1000000 | bytes 3014660 | tf_op jit(solution)/shard_map/pallas_call | solution.py:42
  20.8 0.0 collective-permute-done.before1_ref
  20.8 0.0 collective-permute-done.2.swapped_ref
  20.9 0.0 copy-start.1
  20.9 0.0 copy-start.2
  20.9 3.1 %shard_map.105 = bf16[64,128]{1,0:T(8,128)(2,1)S(1)} custom-call(s32[1]{0:T(128)} %bitcast.role_ref, bf16[64,128]{1,0:T(8,128)(2,1)S(1)} %collective-permute-done.before1_ref, bf16[64,128]{1,0:T(8,128)(2,1)S(1)} %collective-permute-done.1.fetched_ref, bf16[64,128]{1,0:T(8,128)(2,1)S(1)} %collective-permute-done.2.swapped_ref, ...), custom_call_target="tpu_custom_call" | custom-call | flops 3000000000 | bytes 3276804 | tf_op jit(solution)/shard_map/pallas_call | solution.py:42
  24.0 6.9 %all-gather.1 = bf16[256,128]{1,0:T(8,128)(2,1)S(1)} all-gather(bf16[64,128]{1,0:T(8,128)(2,1)S(1)} %shard_map.105), channel_id=3, replica_groups=mesh['role'=4,'seq'=128] {'role'}, dimensions={0}, use_global_device_ids=true | all-gather | bytes 81920 | tf_op jit(solution)/shard_map/all_gather | solution.py:296
  31.0 0.9 %shard_map.106 = (f32[64,128]{1,0:T(8,128)S(1)}, bf16[64,128]{1,0:T(8,128)(2,1)S(1)}, bf16[768,128]{1,0:T(8,128)(2,1)}) custom-call(bf16[4,64,128]{2,1,0:T(8,128)(2,1)S(1)} %bitcast.15, f32[1,128]{1,0:T(1,128)S(1)} %get-tuple-element.28.inv_ref, bf16[768,256]{1,0:T(8,128)(2,1)S(1)} %get-tuple-element.29.spread_ref), custom_call_target="tpu_custom_call" | custom-call | bytes 459264 | tf_op jit(solution)/shard_map/pallas_call | solution.py:42
  31.9 17.3 %all-to-all-start = ((bf16[128,3,2,128]{3,2,1,0:T(2,128)(2,1)}), bf16[128,3,2,128]{3,2,1,0:T(2,128)(2,1)S(1)}, u32[]{:S(2)}, u32[]{:S(2)}) async-start(bf16[128,3,2,128]{3,2,1,0:T(2,128)(2,1)} %bitcast.9), calls=%async_computation | async-start | bytes 393216 | tf_op jit(solution)/shard_map/all_to_all | solution.py:305
  49.2 0.0 copy-done.1
  49.2 0.1 constant_dynamic-slice_fusion
  49.3 0.1 copy.13.head_ref
  49.4 0.0 copy-done.2
  49.4 0.1 dynamic-slice_bitcast_fusion
  49.5 0.1 copy.12.gain_ref
  49.6 1.0 %shard_map.107 = (bf16[128,1280]{1,0:T(8,128)(2,1)}, bf16[64,128]{1,0:T(8,128)(2,1)}) custom-call(f32[64,128]{1,0:T(8,128)S(1)} %get-tuple-element.30.gap_ref, f32[64,128]{1,0:T(8,128)S(1)} %get-tuple-element.31.proj_ref, f32[1,128]{1,0:T(1,128)S(1)} %get-tuple-element.28.inv_ref, bf16[64,128]{1,0:T(8,128)(2,1)S(1)} %get-tuple-element.32.scaled_ref, ...), custom_call_target="tpu_custom_call" | custom-call | flops 1000000000 | bytes 579072 | tf_op jit(solution)/shard_map/pallas_call | solution.py:42
  50.6 12.4 %all-to-all-done = bf16[128,3,2,128]{3,2,1,0:T(2,128)(2,1)S(1)} async-done(((bf16[128,3,2,128]{3,2,1,0:T(2,128)(2,1)}), bf16[128,3,2,128]{3,2,1,0:T(2,128)(2,1)S(1)}, u32[]{:S(2)}, u32[]{:S(2)}) %all-to-all-start) | async-done | bytes 196640 | tf_op jit(solution)/shard_map/all_to_all | solution.py:305
  63.0 0.9 %shard_map.108 = (f32[10,64]{1,0:T(8,128)}, f32[1,10]{1,0:T(1,128)}) custom-call(bf16[768,128]{1,0:T(8,128)(2,1)S(1)} %bitcast.14, f32[10,1]{1,0:T(8,128)S(1)} %copy.12.gain_ref, bf16[10,64]{1,0:T(8,128)(2,1)S(1)} %copy.13.head_ref), custom_call_target="tpu_custom_call" | custom-call | bytes 197928 | tf_op jit(solution)/shard_map/pallas_call | solution.py:42
  (1 shorter events, 0.0 us)
Async XLA Ops:
  12.2 7.7 %copy-start = (bf16[1,4,64,5120]{3,2,1,0:T(8,128)(2,1)S(1)}, bf16[1,4,64,5120]{3,2,1,0:T(8,128)(2,1)}, u32[]{:S(2)}) copy-start(bf16[1,4,64,5120]{3,2,1,0:T(8,128)(2,1)} %w_ref.3) | copy-start | bytes 7864324
  12.3 4.4 %collective-permute-start.1 = (bf16[64,128]{1,0:T(8,128)(2,1)S(1)}, bf16[64,128]{1,0:T(8,128)(2,1)S(1)}, u32[]{:S(2)}, u32[]{:S(2)}) collective-permute-start(bf16[64,128]{1,0:T(8,128)(2,1)S(1)} %get-tuple-element.23.own_ref), channel_id=1, source_target_pairs={{0,2},{1,3},{2,4},{3,5},{4,6},{5,7},{6,8},{7,9},{8,10},{9,11},{10,... | collective-permute-start | bytes 49160 | tf_op jit(solution)/shard_map/ppermute | solution.py:33
  13.7 7.2 %collective-permute-start = (bf16[64,128]{1,0:T(8,128)(2,1)S(1)}, bf16[64,128]{1,0:T(8,128)(2,1)S(1)}, u32[]{:S(2)}, u32[]{:S(2)}) collective-permute-start(bf16[64,128]{1,0:T(8,128)(2,1)S(1)} %get-tuple-element.23.own_ref), channel_id=1, source_target_pairs={{0,1},{1,2},{2,3},{3,4},{4,5},{5,6},{6,7},{7,8},{8,9},{9,10},{10,1... | collective-permute-start | bytes 49160 | tf_op jit(solution)/shard_map/ppermute | solution.py:33
  16.6 4.2 %collective-permute-start.2 = (bf16[64,128]{1,0:T(8,128)(2,1)S(1)}, bf16[64,128]{1,0:T(8,128)(2,1)S(1)}, u32[]{:S(2)}, u32[]{:S(2)}) collective-permute-start(bf16[64,128]{1,0:T(8,128)(2,1)S(1)} %collective-permute-done.1.fetched_ref), channel_id=1, source_target_pairs={{0,128},{1,129},{2,130},{3,131},{4,132},{5,133},{6,134},{7,135},{8... | collective-permute-start | bytes 49160 | tf_op jit(solution)/shard_map/ppermute | solution.py:33
  20.9 28.4 %copy-start.1 = (bf16[1280,64]{0,1:T(8,128)(2,1)S(1)}, bf16[1280,64]{0,1:T(8,128)(2,1)}, u32[]{:S(2)}) copy-start(bf16[1280,64]{0,1:T(8,128)(2,1)} %param.9) | copy-start | bytes 491524
  20.9 28.5 %copy-start.2 = (f32[1280]{0:T(1024)S(1)}, f32[1280]{0:T(1024)}, u32[]{:S(2)}) copy-start(f32[1280]{0:T(1024)} %param.8) | copy-start | bytes 15364
  31.9 31.1 %all-to-all-start = ((bf16[128,3,2,128]{3,2,1,0:T(2,128)(2,1)}), bf16[128,3,2,128]{3,2,1,0:T(2,128)(2,1)S(1)}, u32[]{:S(2)}, u32[]{:S(2)}) async-start(bf16[128,3,2,128]{3,2,1,0:T(2,128)(2,1)} %bitcast.9), calls=%async_computation | async-start | bytes 393216 | tf_op jit(solution)/shard_map/all_to_all | solution.py:305
